TPU v7x, 32 devices: a whole 2x2x4 slice. The times are simulated.
32 devices in a mesh: pole: 2 (over y), row: 4 (over z), col: 2 (over x), sub: 2 (over core).
Axes of the slice: x: 2, y: 2, z: 4, core: 2. Of those that a mesh axis runs over, the one named last changes fastest.
Arguments:
- sep_inverse: bfloat16 [8192, 4096], P(('pole', 'row', 'sub'), 'col'), parts along dimension 0, as said below
- parent_panel: bfloat16 [4, 4096, 1024], P(('pole', 'sub'), 'col'), parts along dimension 0, may hold values from -0.09375 to 0.09375
- parent_pivot: float32 [4, 1024, 1024], P(('pole', 'sub'), None, 'col'), parts along dimension 0, as said below
- parent_cols: int32 [2], replicated, may hold values from 1 to 8, as said below
- parent_blocks: int32 [2, 32], replicated, may hold values 0 or 1
- child_separator: bfloat16 [32, 1024, 512], P(('pole', 'row', 'sub'), 'col'), parts along dimension 0, may hold values from -0.1875 to 0.1875
- child_parent: bfloat16 [32, 1024, 512], P(('pole', 'row', 'sub'), 'col'), parts along dimension 0, may hold values from -0.1875 to 0.1875
- child_pivot: float32 [32, 512, 512], P(('pole', 'row', 'sub'), 'col'), parts along dimension 0, as said below
- child_cols: int32 [16], replicated, may hold values from 1 to 4, as said below
- child_blocks: int32 [16, 8], replicated, may hold values from 0 to 31, as said below
Outputs:
- parent_inverse: float32 [4, 1024, 1024], P(('pole', 'sub'), None, 'col'), parts along dimension 0
- parent_upper: float32 [4, 1024, 4096], P(('pole', 'sub'), 'col', 'row'), parts along dimension 0
- child_inverse: float32 [32, 512, 512], P(('pole', 'row', 'sub'), 'col'), parts along dimension 0
There are 2 independent parts, one for each index of `pole`. A program takes and returns all parts, laid end to end along the dimension named above; an argument that names none is the same for every part. Nothing has to cross between parts.
Inputs may be any that keep to these rules, and one draw needn't show every extreme that they name: `parent_cols`: widths of the first-level supernodes in blocks of 128 columns; some supernode has 8. `child_cols`: widths of the second-level supernodes in blocks of 128 columns; some supernode has 4. `child_blocks`: each row holds 8 distinct block numbers in increasing order. `sep_inverse`: symmetric. `parent_pivot`: each block symmetric. `child_pivot`: each block symmetric.
All inputs are finite; a program needn't handle non-finite values.
Results may differ from a plain program's by a relative error of at most 0.0019.
Values may be sent and summed in bfloat16 or wider, within the bound.
A program may use at most 128 MiB of HBM per device.

v0:
```python
import jax
import jax.numpy as jnp
from jax import lax
from jax.sharding import PartitionSpec as P

BLK = 128
NA = 4096
W1 = 1024
W2 = 512
P2A = 8
CHILD = 2


def spread_2(value, axis, source):
    kept = jnp.where(lax.axis_index(axis) == source, value, 0).astype(value.dtype)
    return lax.psum(kept, axis)


def per_device(
    sep_inverse,
    parent_panel,
    parent_pivot,
    parent_cols,
    parent_blocks,
    child_separator,
    child_parent,
    child_pivot,
    child_cols,
    child_blocks,
):
    rows_count = lax.axis_size("row")
    cols_count = lax.axis_size("col")
    subs_count = lax.axis_size("sub")
    row_at = lax.axis_index("row")
    col_at = lax.axis_index("col")
    sub_at = lax.axis_index("sub")
    strip_len = NA // cols_count
    band_len = NA // rows_count
    slice_one = W1 // cols_count
    slice_two = W2 // cols_count
    zero_value = jnp.zeros((), jnp.bfloat16)
    whole_strip = lax.all_gather(sep_inverse, ("row", "sub"), axis=0, tiled=True)
    own_rows = lax.dynamic_slice_in_dim(whole_strip, row_at * band_len, band_len, 0)
    count_one = lax.dynamic_index_in_dim(parent_cols, sub_at, 0, keepdims=False)
    blocks_one = lax.dynamic_index_in_dim(parent_blocks, sub_at, 0, keepdims=False)
    live_rows = jnp.broadcast_to(blocks_one[:, None] > 0, (NA // BLK, BLK)).reshape(NA)
    strip_live = lax.dynamic_slice_in_dim(live_rows, col_at * strip_len, strip_len, 0)
    live_one = jnp.arange(W1, dtype=jnp.int32) < count_one * BLK
    panel_one = jnp.where(strip_live[:, None] & live_one[None, :], parent_panel[0], zero_value)
    far_block = lax.psum_scatter(
        lax.dot_general(
            panel_one, own_rows, (((0,), (1,)), ((), ())), preferred_element_type=jnp.float32
        ),
        "col",
        scatter_dimension=0,
        tiled=True,
    )
    far_round = far_block.astype(jnp.bfloat16)
    root_col = row_at * cols_count // rows_count
    offset = jnp.clip(row_at * band_len - root_col * strip_len, 0, strip_len - band_len)
    sent_rows = lax.dynamic_slice_in_dim(panel_one, offset, band_len, 0)
    mine_rows = spread_2(sent_rows, "col", root_col)
    partial_value = lax.dot_general(
        mine_rows, far_round, (((0,), (1,)), ((), ())), preferred_element_type=jnp.float32
    )
    summed = lax.psum(partial_value, "row")
    keep_cols = lax.dynamic_slice_in_dim(live_one, col_at * slice_one, slice_one, 0)
    pivot_one = jnp.where(live_one[:, None] & keep_cols[None, :], parent_pivot[0], jnp.float32(0.0))
    inverse_one = pivot_one + summed
    inverse_round = inverse_one.astype(jnp.bfloat16)
    far_all = lax.all_gather(far_round, "row", axis=1, tiled=True)
    side_rows, upper_rows = (
        lax.all_gather(child_separator, "col", axis=1, tiled=True),
        lax.all_gather(child_parent, "col", axis=1, tiled=True),
    )
    first_kid = (row_at * subs_count + sub_at) * CHILD
    kid_cols = lax.dynamic_slice_in_dim(child_cols, first_kid, CHILD, 0)
    kid_blocks = lax.dynamic_slice_in_dim(child_blocks, first_kid, CHILD, 0)
    live_two = jnp.arange(W2, dtype=jnp.int32)[None, :] < kid_cols[:, None] * BLK
    left_side = jnp.where(live_two[:, None, :], side_rows, zero_value)
    right_side = jnp.where(live_two[:, None, :], upper_rows, zero_value)
    picked_rows = (
        kid_blocks[:, :, None] * BLK + jnp.arange(BLK, dtype=jnp.int32)[None, None, :]
    ).reshape(CHILD, P2A * BLK)
    chosen = jnp.take(whole_strip, picked_rows, axis=0)
    left_sep = jnp.einsum(
        "kpw,kps->kws", left_side, chosen, preferred_element_type=jnp.float32
    ).astype(jnp.bfloat16)
    strip_blocks = col_at * (strip_len // BLK) + jnp.arange(strip_len // BLK, dtype=jnp.int32)
    block_hits = (kid_blocks[:, None, :] == strip_blocks[None, :, None]).astype(jnp.bfloat16)
    spread = jnp.einsum(
        "kbp,kpiw->kbiw",
        block_hits,
        left_side.reshape(CHILD, P2A, BLK, W2),
        preferred_element_type=jnp.float32,
    )
    spread = spread.astype(jnp.bfloat16).reshape(CHILD, strip_len, W2)
    cross_rows = jnp.take(far_all, picked_rows, axis=1)
    left_cross = jnp.einsum(
        "kpw,jkp->kwj", left_side, cross_rows, preferred_element_type=jnp.float32
    ).astype(jnp.bfloat16)
    left_par = jnp.einsum(
        "kjw,jc->kwc", right_side, inverse_round, preferred_element_type=jnp.float32
    ).astype(jnp.bfloat16)
    right_slice = lax.dynamic_slice_in_dim(right_side, col_at * slice_one, slice_one, 1)
    term_sum = jnp.einsum("kws,ksv->wkv", left_sep, spread, preferred_element_type=jnp.float32)
    term_sum = term_sum + jnp.einsum(
        "kwc,kcv->wkv", left_par, right_slice, preferred_element_type=jnp.float32
    )
    term_sum = term_sum - jnp.einsum(
        "kwj,kjv->wkv", left_cross, right_slice, preferred_element_type=jnp.float32
    )
    term_sum = term_sum - jnp.einsum(
        "kvj,kjw->wkv", left_cross, right_slice, preferred_element_type=jnp.float32
    )
    summed_two = lax.psum_scatter(term_sum, "col", scatter_dimension=0, tiled=True)
    keep_two = lax.dynamic_slice_in_dim(live_two, col_at * slice_two, slice_two, 1)
    pivot_two = jnp.where(
        keep_two[:, :, None] & live_two[:, None, :], child_pivot, jnp.float32(0.0)
    )
    child_out = pivot_two + jnp.transpose(summed_two, (1, 0, 2))
    return (inverse_one[None], (-far_block)[None], child_out)


def solution(mesh):
    return jax.shard_map(
        per_device,
        mesh=mesh,
        in_specs=(
            P(("pole", "row", "sub"), "col"),
            P(("pole", "sub"), "col", None),
            P(("pole", "sub"), None, "col"),
            P(),
            P(),
            P(("pole", "row", "sub"), "col", None),
            P(("pole", "row", "sub"), "col", None),
            P(("pole", "row", "sub"), "col", None),
            P(),
            P(),
        ),
        out_specs=(
            P(("pole", "sub"), None, "col"),
            P(("pole", "sub"), "col", "row"),
            P(("pole", "row", "sub"), "col", None),
        ),
        check_vma=False,
    )
```

profile of v0, /device:TPU:0, one launch (start us, length us, event | category | flops | bytes accessed | tf_op | source)
XLA Modules:
  0.0 610.8 jit_solution(8212281381414646984)
XLA Ops:
  9.3 4.3 and_select_fusion
  13.7 149.8 %all-gather.5.cloned.1.call-done = bf16[4096,2048]{1,0:T(8,128)(2,1)} async-done(((bf16[512,2048]{1,0:T(8,128)(2,1)}), bf16[4096,2048]{1,0:T(8,128)(2,1)}) %all-gather.5.cloned.1.call-update) | async-done | bytes 16777232 | tf_op jit(solution)/shard_map/all_gather | solution.py:42
  163.5 9.9 %fusion.11 = f32[1024,1024]{1,0:T(8,128)} fusion(bf16[2048,1024]{1,0:T(8,128)(2,1)} %and_select_fusion, bf16[4096,2048]{1,0:T(8,128)(2,1)} %all-gather.5.cloned.1.call-done, s32[]{:T(128)S(6)} %select_n.90), kind=kOutput, calls=%fused_computation.9 | convolution fusion | flops 4294967296 | bytes 12582916 | tf_op jit(solution)/shard_map/dot_general | solution.py:51
  173.5 3.6 dynamic-slice_select_fusion
  181.4 44.7 %reduce-scatter.3.cloned.1.call-done = f32[512,1024]{1,0:T(8,128)} async-done(((f32[1024,1024]{1,0:T(8,128)}), f32[512,1024]{1,0:T(8,128)}) %reduce-scatter.3.cloned.1.call-update) | async-done | bytes 2097168 | tf_op jit(solution)/shard_map/reduce_scatter | solution.py:50
  226.1 4.1 negate_bitcast_fusion
  230.2 61.9 %all-reduce.3.cloned.1.call-done = bf16[1024,1024]{1,0:T(8,128)(2,1)} async-done(((bf16[1024,1024]{1,0:T(8,128)(2,1)}), bf16[1024,1024]{1,0:T(8,128)(2,1)}) %all-reduce.3.cloned.1.call-update) | async-done | bytes 2097168 | tf_op jit(solution)/shard_map/psum | solution.py:16
  292.0 4.2 fusion.54
  297.8 28.8 %all-gather.7.cloned.1.call-done = bf16[2,1024,512]{1,2,0:T(8,128)(2,1)} async-done(((bf16[2,512,512]{1,2,0:T(8,128)(2,1)}), bf16[2,1024,512]{1,2,0:T(8,128)(2,1)}) %all-gather.7.cloned.1.call-update) | async-done | bytes 2097168 | tf_op jit(solution)/shard_map/all_gather | solution.py:73
  326.6 35.1 %all-gather.9.cloned.1.call-done = bf16[2,1024,512]{1,2,0:T(8,128)(2,1)} async-done(((bf16[2,512,512]{1,2,0:T(8,128)(2,1)}), bf16[2,1024,512]{1,2,0:T(8,128)(2,1)}) %all-gather.9.cloned.1.call-update) | async-done | bytes 2097168 | tf_op jit(solution)/shard_map/all_gather | solution.py:74
  361.7 4.0 broadcast_select_fusion
  367.6 5.0 copy.25
  372.6 2.9 convolution_convert_fusion
  375.6 4.3 copy.26
  379.9 24.4 %gather_fusion = bf16[2048,2048]{1,0:T(8,128)(2,1)} fusion(bf16[4096,2048]{1,0:T(8,128)(2,1)} %all-gather.5.cloned.1.call-done, s32[2048]{0:T(1024)S(1)} %bitcast_clamp_fusion), kind=kCustom, calls=%fused_computation | custom fusion | bytes 16785408 | tf_op jit(solution)/shard_map/jit(_take)/gather | solution.py:85
  404.3 46.8 %all-reduce.5.cloned.1.call-done = f32[1024,512]{1,0:T(8,128)} async-done(((f32[1024,512]{1,0:T(8,128)}), f32[1024,512]{1,0:T(8,128)}) %all-reduce.5.cloned.1.call-update) | async-done | bytes 2097168 | tf_op jit(solution)/shard_map/psum | solution.py:66
  451.1 6.4 %fusion.28 = f32[2,512,512]{2,1,0:T(8,128)} fusion(bf16[2,1024,512]{1,2,0:T(8,128)(2,1)} %get-tuple-element.13, s32[]{:T(128)S(6)} %select_n.83, f32[1024,512]{1,0:T(8,128)} %all-reduce.5.cloned.1.call-done, f32[1,1024,512]{2,1,0:T(8,128)} %param.12, pred[512]{0:T(512)(128)(4,1)S(1)} %dynamic_slice.33, pred[1024]{0:T(1024)(128)(4,1)S(1)} %iota_compare_fusion.1), kind=kOutput, calls=%fused_computation.26 | convolution fusion | flops 1613234176 | bytes 9438724 | tf_op jit(solution)/shard_map/kwc,kcv->wkv/dot_general | solution.py:107
  457.5 75.0 %all-gather.11.cloned.1.call-done = bf16[512,4096]{1,0:T(8,128)(2,1)} async-done(((bf16[512,1024]{1,0:T(8,128)(2,1)}), bf16[512,4096]{1,0:T(8,128)(2,1)}) %all-gather.11.cloned.1.call-update) | async-done | bytes 4194320 | tf_op jit(solution)/shard_map/all_gather | solution.py:71
  532.5 6.5 %copy.30 = bf16[512,4096]{0,1:T(8,128)(2,1)} copy(bf16[512,4096]{1,0:T(8,128)(2,1)} %all-gather.11.cloned.1.call-done) | data formatting | bytes 8388608 | tf_op jit(solution)/shard_map/all_gather | solution.py:71
  538.9 12.0 %gather_fusion.1 = bf16[2048,512]{1,0:T(8,128)(2,1)} fusion(bf16[512,4096]{0,1:T(8,128)(2,1)} %copy.30, s32[2048]{0:T(1024)S(1)} %bitcast_clamp_fusion), kind=kCustom, calls=%fused_computation.1 | custom fusion | bytes 4202496 | tf_op jit(solution)/shard_map/jit(_take)/gather | solution.py:98
  550.9 5.1 fusion.26
  558.9 11.7 %bitcast_subtract_fusion = f32[512,2,512]{0,2,1:T(8,128)} fusion(f32[2,512,512]{1,2,0:T(8,128)} %copy.31, f32[2,512,512]{2,1,0:T(8,128)} %fusion.26, f32[2,512,512]{2,1,0:T(8,128)} %fusion.28, bf16[2,2048,512]{2,1,0:T(8,128)(2,1)} %bitcast.76, bf16[2,1024,512]{1,2,0:T(8,128)(2,1)S(1)} %get-tuple-element.14, bf16[2,1024,2048]{2,1,0:T(8,128)(2,1)} %bitcast.73, ...), kind=kOutput, calls=%fused_computation.12 | convolution fusion | flops 6450315264 | bytes 23070720 | tf_op jit(solution)/shard_map/kws,ksv->wkv/dot_general | solution.py:106
  572.5 3.3 fusion.39
  575.8 25.4 %reduce-scatter.5.cloned.1.call-done = f32[256,2,512]{0,2,1:T(8,128)} async-done(((f32[512,2,512]{0,2,1:T(8,128)}), f32[256,2,512]{0,2,1:T(8,128)}) %reduce-scatter.5.cloned.1.call-update) | async-done | bytes 1048592 | tf_op jit(solution)/shard_map/reduce_scatter | solution.py:116
  (59 shorter events, 16.7 us)
Async XLA Ops:
  7.2 0.8 copy-start.6
  7.2 2.1 copy-start.5
  7.2 156.3 %all-gather.5.cloned.1.call-start = ((), (), s32[]{:S(2)}) async-start(), calls=%async_computation.3 | async-start | bytes 18874368 | tf_op jit(solution)/shard_map/all_gather | solution.py:42
  7.9 218.2 %reduce-scatter.3.cloned.1.call-start = ((), (), s32[]{:S(2)}) async-start(), calls=%async_computation.4 | async-start | bytes 6291456 | tf_op jit(solution)/shard_map/reduce_scatter | solution.py:50
  173.4 118.6 %all-reduce.3.cloned.1.call-start = ((), (), s32[]{:S(2)}) async-start(), calls=%async_computation.2 | async-start | bytes 4194304 | tf_op jit(solution)/shard_map/psum | solution.py:16
  177.1 1.5 copy-start.2
  177.1 2.9 copy-start.3
  177.1 149.5 %all-gather.7.cloned.1.call-start = ((), (), s32[]{:S(2)}) async-start(), calls=%async_computation.6 | async-start | bytes 3145728 | tf_op jit(solution)/shard_map/all_gather | solution.py:73
  180.0 181.7 %all-gather.9.cloned.1.call-start = ((), (), s32[]{:S(2)}) async-start(), calls=%async_computation.7 | async-start | bytes 3145728 | tf_op jit(solution)/shard_map/all_gather | solution.py:74
  181.4 269.7 %all-reduce.5.cloned.1.call-start = ((), (), s32[]{:S(2)}) async-start(), calls=%async_computation.5 | async-start | bytes 4194304 | tf_op jit(solution)/shard_map/psum | solution.py:66
  230.2 66.1 %copy-start = (bf16[512,1024]{1,0:T(8,128)(2,1)}, bf16[512,1024]{1,0:T(8,128)(2,1)S(1)}, u32[]{:S(2)}) copy-start(bf16[512,1024]{1,0:T(8,128)(2,1)S(1)} %get-tuple-element.12) | copy-start | bytes 3145732
  296.3 0.9 copy-start.4
  296.3 1.2 copy-start.7
  296.3 236.2 %all-gather.11.cloned.1.call-start = ((), (), s32[]{:S(2)}) async-start(), calls=%async_computation.8 | async-start | bytes 5242880 | tf_op jit(solution)/shard_map/all_gather | solution.py:71
  297.0 304.1 %reduce-scatter.5.cloned.1.call-start = ((), (), s32[]{:S(2)}) async-start(), calls=%async_computation.9 | async-start | bytes 3145728 | tf_op jit(solution)/shard_map/reduce_scatter | solution.py:116
  570.6 1.9 copy-start.1
Sparse Core Ops, SparseCore 0:
  9.6 153.7 all-gather.4
  173.5 52.5 reduce-scatter.2
  229.1 62.9 all-reduce.2
  293.4 33.1 all-gather.6
  328.6 33.1 all-gather.8
  364.5 86.5 all-reduce.4
  452.7 79.7 all-gather.10
  570.8 30.3 reduce-scatter.4
where the time goes:
time: 611 us
  waiting for transfers between devices  469 us (77%)
  local copies, waits for them, and re-layouts  65.3 us (11%)
  matrix products  40.4 us (7%)
  other arithmetic  20.9 us (3%)
  between operations  15 us (2%)
    all_gather x1, waiting for transfers between devices, per_device(): lax.all_gather(sep_inverse, ('row', 'sub'), axis=0, tiled=True)  150 us
    all_gather x1, waiting for transfers between devices, per_device(): far_all = lax.all_gather(far_round, 'row', axis=1, tiled=True)  75 us
    psum x1, waiting for transfers between devices, spread_2(): return lax.psum(kept, axis)  61.9 us
    psum x1, waiting for transfers between devices, per_device(): summed = lax.psum(partial_value, 'row')  46.8 us
    reduce_scatter x1, waiting for transfers between devices, per_device(): lax.psum_scatter(lax.dot_general(panel_one, own_rows, (((0,), (1,)), ((),...  44.7 us
    all_gather x1, waiting for transfers between devices, per_device(): lax.all_gather(child_parent, 'col', axis=1, tiled=True)  35.1 us
    all_gather x1, waiting for transfers between devices, per_device(): lax.all_gather(child_separator, 'col', axis=1, tiled=True)  28.8 us
    reduce_scatter x1, waiting for transfers between devices, per_device(): lax.psum_scatter(term_sum, 'col', scatter_dimension=0, tiled=True)  25.4 us
  transfers between devices with their start and end apart: 8, of which 8 were waited for; matrix products, arithmetic and copies ran while one was open for 12% of the time, Pallas kernels for 0%

commit v1 on v0

v1 whole, which is shorter than its diff:
```python
import jax
import jax.numpy as jnp
from jax import lax
from jax.sharding import PartitionSpec as P

BLK = 128
P2A = 8
CHILD = 2
BF = jnp.bfloat16
F32 = jnp.float32


def swap(value, axis):
    return lax.ppermute(value, axis, [(0, 1), (1, 0)])


def spread_2(value, axis, source):
    kept = jnp.where(lax.axis_index(axis) == source, value, 0).astype(value.dtype)
    return lax.psum(kept, axis)


def pair_gather(value, axis, dim):
    if lax.axis_size(axis) != 2:
        return lax.all_gather(value, axis, axis=dim, tiled=True)
    other = swap(value, axis)
    first = lax.axis_index(axis) == 0
    return jnp.concatenate(
        [jnp.where(first, value, other), jnp.where(first, other, value)], axis=dim
    )


def pair_scatter(value, axis):
    if lax.axis_size(axis) != 2:
        return lax.psum_scatter(value, axis, scatter_dimension=0, tiled=True)
    half = value.shape[0] // 2
    at = lax.axis_index(axis)
    sent = lax.dynamic_slice_in_dim(value, (1 - at) * half, half, 0)
    kept = lax.dynamic_slice_in_dim(value, at * half, half, 0)
    return kept + swap(sent, axis)


def dot(a, b, dims):
    return lax.dot_general(a, b, (dims, ((), ())), preferred_element_type=F32)


def per_device(
    sep_inverse,
    parent_panel,
    parent_pivot,
    parent_cols,
    parent_blocks,
    child_separator,
    child_parent,
    child_pivot,
    child_cols,
    child_blocks,
):
    rows_count = lax.axis_size("row")
    cols_count = lax.axis_size("col")
    subs_count = lax.axis_size("sub")
    row_at = lax.axis_index("row")
    col_at = lax.axis_index("col")
    sub_at = lax.axis_index("sub")
    strip_len = sep_inverse.shape[1]
    order = strip_len * cols_count
    band_len = order // rows_count
    w1 = parent_panel.shape[2]
    w2 = child_separator.shape[2]
    slice_one = w1 // cols_count
    slice_two = w2 // cols_count
    zero = jnp.zeros((), BF)

    whole_strip = lax.all_gather(sep_inverse, ("row", "sub"), axis=0, tiled=True)
    own_rows = pair_gather(sep_inverse, "sub", 0)

    count_one = lax.dynamic_index_in_dim(parent_cols, sub_at, 0, keepdims=False)
    blocks_one = lax.dynamic_index_in_dim(parent_blocks, sub_at, 0, keepdims=False)
    live_rows = jnp.broadcast_to(blocks_one[:, None] > 0, (order // BLK, BLK)).reshape(order)
    strip_live = lax.dynamic_slice_in_dim(live_rows, col_at * strip_len, strip_len, 0)
    live_one = jnp.arange(w1, dtype=jnp.int32) < count_one * BLK
    panel_one = jnp.where(strip_live[:, None] & live_one[None, :], parent_panel[0], zero)

    root_col = row_at * cols_count // rows_count
    offset = jnp.clip(row_at * band_len - root_col * strip_len, 0, strip_len - band_len)
    sent_rows = lax.dynamic_slice_in_dim(panel_one, offset, band_len, 0)
    if cols_count == 2:
        mine_rows = jnp.where(col_at == root_col, sent_rows, swap(sent_rows, "col"))
    else:
        mine_rows = spread_2(sent_rows, "col", root_col)
    far_block = pair_scatter(dot(panel_one, own_rows, ((0,), (1,))), "col")
    far_round = far_block.astype(BF)
    partial_value = dot(mine_rows, far_round, ((0,), (1,)))
    summed = lax.psum(partial_value, "row")
    keep_cols = lax.dynamic_slice_in_dim(live_one, col_at * slice_one, slice_one, 0)
    pivot_one = jnp.where(live_one[:, None] & keep_cols[None, :], parent_pivot[0], F32(0.0))
    inverse_one = pivot_one + summed
    inverse_round = inverse_one.astype(BF)

    side_rows = pair_gather(child_separator, "col", 1)
    upper_rows = pair_gather(child_parent, "col", 1)
    first_kid = (row_at * subs_count + sub_at) * CHILD
    kid_cols = lax.dynamic_slice_in_dim(child_cols, first_kid, CHILD, 0)
    kid_blocks = lax.dynamic_slice_in_dim(child_blocks, first_kid, CHILD, 0)
    live_two = jnp.arange(w2, dtype=jnp.int32)[None, :] < kid_cols[:, None] * BLK
    left_side = jnp.where(live_two[:, None, :], side_rows, zero)
    right_side = jnp.where(live_two[:, None, :], upper_rows, zero)
    strip_blocks = col_at * (strip_len // BLK) + jnp.arange(strip_len // BLK, dtype=jnp.int32)
    block_hits = (kid_blocks[:, None, :] == strip_blocks[None, :, None]).astype(BF)
    spread = jnp.einsum(
        "kbp,kpiw->kbiw",
        block_hits,
        left_side.reshape(CHILD, P2A, BLK, w2),
        preferred_element_type=F32,
    )
    spread = spread.astype(BF).reshape(CHILD, strip_len, w2)

    picked_rows = (
        kid_blocks[:, :, None] * BLK + jnp.arange(BLK, dtype=jnp.int32)[None, None, :]
    ).reshape(CHILD, P2A * BLK)

    terms = []
    for k in range(CHILD):
        right_slice = lax.dynamic_slice_in_dim(right_side[k], col_at * slice_one, slice_one, 0)
        left_par = dot(right_side[k], inverse_round, ((0,), (0,))).astype(BF)
        par_term = dot(left_par, right_slice, ((1,), (0,)))
        reach = dot(panel_one, right_side[k], ((1,), (0,))).astype(BF)
        chosen = jnp.take(whole_strip, picked_rows[k], axis=0)
        weight = dot(left_side[k], chosen, ((0,), (0,))).astype(BF)
        sep_term = dot(weight, spread[k], ((1,), (0,)))
        cross = dot(weight, reach, ((1,), (0,)))
        terms.append(sep_term + par_term - cross - cross.T)
    term_sum = jnp.stack(terms, axis=1)
    summed_two = pair_scatter(term_sum, "col")
    keep_two = lax.dynamic_slice_in_dim(live_two, col_at * slice_two, slice_two, 1)
    pivot_two = jnp.where(keep_two[:, :, None] & live_two[:, None, :], child_pivot, F32(0.0))
    child_out = pivot_two + jnp.transpose(summed_two, (1, 0, 2))
    return (inverse_one[None], (-far_block)[None], child_out)


def solution(mesh):
    return jax.shard_map(
        per_device,
        mesh=mesh,
        in_specs=(
            P(("pole", "row", "sub"), "col"),
            P(("pole", "sub"), "col", None),
            P(("pole", "sub"), None, "col"),
            P(),
            P(),
            P(("pole", "row", "sub"), "col", None),
            P(("pole", "row", "sub"), "col", None),
            P(("pole", "row", "sub"), "col", None),
            P(),
            P(),
        ),
        out_specs=(
            P(("pole", "sub"), None, "col"),
            P(("pole", "sub"), "col", "row"),
            P(("pole", "row", "sub"), "col", None),
        ),
        check_vma=False,
    )
```

time: 611 us -> 448 us (0.73)
  waiting for transfers between devices: 469 us -> 297 us
  matrix products: 40.4 us -> 54.7 us
  local copies, waits for them, and re-layouts: 65.3 us -> 51.5 us
  starting transfers between devices: 0.32 us -> 7.56 us
    all_gather x1, waiting for transfers between devices: 150 us -> 0.03 us  [per_device(): lax.all_gather(sep_inverse, ('row', 'sub'), axis=0, tiled=True)]
    ppermute x0 -> x6, waiting for transfers between devices: none -> 143 us  [swap(): return lax.ppermute(value, axis, [(0, 1), (1, 0)])]
    all_gather x3 -> x0, waiting for transfers between devices: 139 us -> none  [the longest x1 75 us: per_device(): far_all = lax.all_gather(far_round, 'row', axis=1, tiled=True)]
    psum x1, waiting for transfers between devices: 46.8 us -> 154 us  [per_device(): summed = lax.psum(partial_value, 'row')]
    reduce_scatter x2 -> x0, waiting for transfers between devices: 70.1 us -> none  [the longest x1 44.7 us: per_device(): lax.psum_scatter(lax.dot_general(panel_one, own_rows, (((0,), (1,)), ((),...]
    psum x1 -> x0, waiting for transfers between devices: 61.9 us -> none  [spread_2(): return lax.psum(kept, axis)]
    dot_general x5 -> x10, matrix products: 37.4 us -> 52.9 us  [dot(): return lax.dot_general(a, b, (dims, ((), ())), preferred_element_type=F32)]
    ppermute x0 -> x6, starting transfers between devices: none -> 7.3 us  [swap(): return lax.ppermute(value, axis, [(0, 1), (1, 0)])]
  transfers between devices with their start and end apart: 8 -> 8, of which waited for: 8 -> 6; matrix products, arithmetic and copies ran while one was open for 12% -> 8% of each run, Pallas kernels for 0% -> 0%
where the time goes in v1:
time: 448 us
  waiting for transfers between devices  297 us (66%)
  matrix products  54.7 us (12%)
  local copies, waits for them, and re-layouts  51.5 us (11%)
  other arithmetic  20.7 us (5%)
  between operations  16.3 us (4%)
  starting transfers between devices  7.56 us (2%)
    psum x1, waiting for transfers between devices, per_device(): summed = lax.psum(partial_value, 'row')  154 us
    ppermute x6, waiting for transfers between devices, swap(): return lax.ppermute(value, axis, [(0, 1), (1, 0)])  143 us
    dot_general x10, matrix products, dot(): return lax.dot_general(a, b, (dims, ((), ())), preferred_element_type=F32)  52.9 us
    gather x2, local copies, waits for them, and re-layouts, per_device(): chosen = jnp.take(whole_strip, picked_rows[k], axis=0)  34.3 us
  transfers between devices with their start and end apart: 8, of which 6 were waited for; matrix products, arithmetic and copies ran while one was open for 8% of the time, Pallas kernels for 0%

profile of v1, /device:TPU:0, one launch (start us, length us, event | category | flops | bytes accessed | tf_op | source)
XLA Modules:
  0.0 447.7 jit_solution(18168084646680862956)
XLA Ops:
  11.2 3.0 and_select_fusion.1
  16.2 2.5 collective-permute-start
  18.7 2.6 broadcast_select_fusion.2
  22.2 4.6 %fusion.1 = f32[1024,1024]{1,0:T(8,128)S(1)} fusion(bf16[2048,1024]{1,0:T(8,128)(2,1)S(1)} %copy-done.2, bf16[512,2048]{1,0:T(8,128)(2,1)S(1)} %get-tuple-element.9, bf16[512,2048]{1,0:T(8,128)(2,1)S(1)} %get-tuple-element.8), kind=kOutput, calls=%fused_computation.5 | convolution fusion | flops 4303355904 | bytes 12582912 | tf_op jit(solution)/shard_map/dot_general | solution.py:43
  29.4 35.9 %collective-permute-done = bf16[1024,1024]{1,0:T(8,128)(2,1)} collective-permute-done((bf16[1024,1024]{1,0:T(8,128)(2,1)S(1)}, bf16[1024,1024]{1,0:T(8,128)(2,1)}, u32[]{:S(2)}, u32[]{:S(2)}) %collective-permute-start) | collective-permute-done | bytes 2097184 | tf_op jit(solution)/shard_map/ppermute | solution.py:14
  65.3 44.7 %collective-permute-done.2 = f32[512,1024]{1,0:T(8,128)} collective-permute-done((f32[512,1024]{1,0:T(8,128)}, f32[512,1024]{1,0:T(8,128)}, u32[]{:S(2)}, u32[]{:S(2)}) %collective-permute-start.2) | collective-permute-done | bytes 2097184 | tf_op jit(solution)/shard_map/ppermute | solution.py:14
  110.0 4.9 %fusion.20 = f32[1024,512]{1,0:T(8,128)} fusion(bf16[1024,1024]{1,0:T(8,128)(2,1)S(1)} %constant_dynamic-slice_fusion.3, bf16[1024,1024]{1,0:T(8,128)(2,1)} %collective-permute-done, pred[]{:T(512)S(6)} %eq.23, f32[512,1024]{1,0:T(8,128)} %collective-permute-done.2, f32[1024,1024]{1,0:T(8,128)} %copy-done.3, s32[]{:T(128)S(6)} %select_n.111), kind=kOutput, calls=%fused_computation.33 | convolution fusion | flops 1075838976 | bytes 10485765 | tf_op jit(solution)/shard_map/dot_general | solution.py:43
  119.4 23.2 %collective-permute-done.3 = bf16[2,512,512]{2,1,0:T(8,128)(2,1)} collective-permute-done((bf16[2,512,512]{2,1,0:T(8,128)(2,1)S(1)}, bf16[2,512,512]{2,1,0:T(8,128)(2,1)}, u32[]{:S(2)}, u32[]{:S(2)}) %collective-permute-start.3) | collective-permute-done | bytes 1048608 | tf_op jit(solution)/shard_map/ppermute | solution.py:14
  144.0 20.0 %collective-permute-done.4 = bf16[2,512,512]{2,1,0:T(8,128)(2,1)S(1)} collective-permute-done((bf16[2,512,512]{2,1,0:T(8,128)(2,1)S(1)}, bf16[2,512,512]{2,1,0:T(8,128)(2,1)S(1)}, u32[]{:S(2)}, u32[]{:S(2)}) %collective-permute-start.4) | collective-permute-done | bytes 1048608 | tf_op jit(solution)/shard_map/ppermute | solution.py:14
  170.9 2.5 copy.23
  174.9 153.6 %all-reduce.2.cloned.1.call-done = f32[1024,512]{1,0:T(8,128)} async-done(((f32[1024,512]{1,0:T(8,128)}), f32[1024,512]{1,0:T(8,128)}) %all-reduce.2.cloned.1.call-update) | async-done | bytes 2097168 | tf_op jit(solution)/shard_map/psum | solution.py:93
  328.5 2.6 fusion.17
  331.1 17.5 %gather_fusion = bf16[1024,2048]{1,0:T(8,128)(2,1)} fusion(bf16[4096,2048]{1,0:T(8,128)(2,1)} %all-gather.2.cloned.1.call-done, s32[1024]{0:T(1024)S(1)} %get-tuple-element.21), kind=kCustom, calls=%fused_computation.clone | custom fusion | bytes 8392704 | tf_op jit(solution)/shard_map/jit(_take)/gather | solution.py:127
  348.6 6.3 %fusion.11 = bf16[512,2048]{1,0:T(8,128)(2,1)} fusion(bf16[1024,2048]{1,0:T(8,128)(2,1)} %gather_fusion, pred[1024]{0:T(1024)(128)(4,1)S(1)} %get-tuple-element.19, bf16[2,1024,512]{2,1,0:T(8,128)(2,1)} %get-tuple-element.13), kind=kOutput, calls=%fused_computation.17 | convolution fusion | flops 2150629376 | bytes 7341056 | tf_op jit(solution)/shard_map/dot_general | solution.py:43
  355.0 6.7 %fusion.48 = f32[512,512]{1,0:T(8,128)S(1)} fusion(bf16[512,2048]{1,0:T(8,128)(2,1)} %fusion.11, bf16[1,2048,1024]{2,1,0:T(8,128)(2,1)} %param.13, pred[1024]{0:T(1024)(128)(4,1)S(1)} %iota_compare_fusion.1, pred[2048]{0:T(1024)(128)(4,1)S(1)} %dynamic_slice.51, bf16[2,1024,512]{2,1,0:T(8,128)(2,1)} %copy-done.5), kind=kOutput, calls=%fused_computation.62 | convolution fusion | flops 3226468352 | bytes 8391680 | tf_op jit(solution)/shard_map/dot_general | solution.py:43
  361.7 4.8 %fusion.88 = f32[512,512]{1,0:T(8,128)} fusion(bf16[512,2048]{1,0:T(8,128)(2,1)} %fusion.11, bf16[2048,512]{1,0:T(8,128)(2,1)} %bitcast.98), kind=kOutput, calls=%fused_computation.113 | convolution fusion | flops 1073741824 | bytes 5242880 | tf_op jit(solution)/shard_map/dot_general | solution.py:43
  367.9 16.8 %gather_fusion.1 = bf16[1024,2048]{1,0:T(8,128)(2,1)} fusion(bf16[4096,2048]{1,0:T(8,128)(2,1)} %all-gather.2.cloned.1.call-done, s32[1024]{0:T(1024)S(1)} %get-tuple-element.20), kind=kCustom, calls=%fused_computation.1.clone | custom fusion | bytes 8392704 | tf_op jit(solution)/shard_map/jit(_take)/gather | solution.py:127
  384.6 6.3 %fusion.14 = bf16[512,2048]{1,0:T(8,128)(2,1)} fusion(bf16[1024,2048]{1,0:T(8,128)(2,1)} %gather_fusion.1, pred[1024]{0:T(1024)(128)(4,1)S(1)} %get-tuple-element.18, bf16[2,1024,512]{2,1,0:T(8,128)(2,1)} %get-tuple-element.13), kind=kOutput, calls=%fused_computation.18 | convolution fusion | flops 2150629376 | bytes 7341056 | tf_op jit(solution)/shard_map/dot_general | solution.py:43
  391.0 6.7 %fusion.41 = f32[512,512]{1,0:T(8,128)S(1)} fusion(bf16[512,2048]{1,0:T(8,128)(2,1)} %fusion.14, bf16[1,2048,1024]{2,1,0:T(8,128)(2,1)} %param.13, pred[1024]{0:T(1024)(128)(4,1)S(1)} %iota_compare_fusion.1, pred[2048]{0:T(1024)(128)(4,1)S(1)} %dynamic_slice.51, bf16[2,1024,512]{2,1,0:T(8,128)(2,1)} %copy-done.5), kind=kOutput, calls=%fused_computation.59 | convolution fusion | flops 3226468352 | bytes 8391680 | tf_op jit(solution)/shard_map/dot_general | solution.py:43
  397.7 4.9 %fusion.89 = f32[512,512]{1,0:T(8,128)} fusion(bf16[512,2048]{1,0:T(8,128)(2,1)} %fusion.14, bf16[2048,512]{1,0:T(8,128)(2,1)} %bitcast.97), kind=kOutput, calls=%fused_computation.114 | convolution fusion | flops 1073741824 | bytes 5242880 | tf_op jit(solution)/shard_map/dot_general | solution.py:43
  403.9 3.3 fusion.29
  407.3 4.3 fusion.26
  414.3 4.3 negate_bitcast_fusion
  418.6 19.2 %collective-permute-done.5 = f32[256,2,512]{2,0,1:T(8,128)} collective-permute-done((f32[256,2,512]{2,0,1:T(8,128)S(1)}, f32[256,2,512]{2,0,1:T(8,128)}, u32[]{:S(2)}, u32[]{:S(2)}) %collective-permute-start.5) | collective-permute-done | bytes 1048608 | tf_op jit(solution)/shard_map/ppermute | solution.py:14
  (66 shorter events, 30.0 us)
Async XLA Ops:
  8.0 320.5 %all-reduce.2.cloned.1.call-start = ((), (), s32[]{:S(2)}) async-start(), calls=%async_computation | async-start | bytes 4194304 | tf_op jit(solution)/shard_map/psum | solution.py:93
  8.0 10.7 %collective-permute-start.1 = (bf16[512,2048]{1,0:T(8,128)(2,1)}, bf16[512,2048]{1,0:T(8,128)(2,1)}, u32[]{:S(2)}, u32[]{:S(2)}) collective-permute-start(bf16[512,2048]{1,0:T(8,128)(2,1)} %param.12), channel_id=1, source_target_pairs={{0,1},{1,0},{2,3},{3,2},{4,5},{5,4},{6,7},{7,6},{8,9},{9,8},{10,11... | collective-permute-start | bytes 6291464 | tf_op jit(solution)/shard_map/ppermute | solution.py:14
  14.2 2.0 copy-start.1
  16.2 49.1 %collective-permute-start = (bf16[1024,1024]{1,0:T(8,128)(2,1)S(1)}, bf16[1024,1024]{1,0:T(8,128)(2,1)}, u32[]{:S(2)}, u32[]{:S(2)}) collective-permute-start(bf16[1024,1024]{1,0:T(8,128)(2,1)S(1)} %constant_dynamic-slice_fusion.3), channel_id=1, source_target_pairs={{0,2},{2,0},{1,3},{3,1},{4,6},{6,4},{5,7},{7,5},{8,10},{10,8},{9,1... | collective-permute-start | bytes 6291464 | tf_op jit(solution)/shard_map/ppermute | solution.py:14
  18.7 3.4 copy-start.2
  26.7 2.7 copy-start.3
  29.4 80.6 %collective-permute-start.2 = (f32[512,1024]{1,0:T(8,128)}, f32[512,1024]{1,0:T(8,128)}, u32[]{:S(2)}, u32[]{:S(2)}) collective-permute-start(f32[512,1024]{1,0:T(8,128)} %constant_dynamic-slice_fusion.2), channel_id=1, source_target_pairs={{0,2},{2,0},{1,3},{3,1},{4,6},{6,4},{5,7},{7,5},{8,10},{10,8},{9,1... | collective-permute-start | bytes 6291464 | tf_op jit(solution)/shard_map/ppermute | solution.py:14
  114.9 1.2 copy-start.8
  114.9 3.6 copy-start.9
  114.9 3.9 copy-start.11
  114.9 4.0 copy-start.12
  114.9 216.2 %all-gather.2.cloned.1.call-start = ((), (), s32[]{:S(2)}) async-start(), calls=%async_computation.1 | async-start | bytes 18874368 | tf_op jit(solution)/shard_map/all_gather | solution.py:73
  116.1 26.5 %collective-permute-start.3 = (bf16[2,512,512]{2,1,0:T(8,128)(2,1)S(1)}, bf16[2,512,512]{2,1,0:T(8,128)(2,1)}, u32[]{:S(2)}, u32[]{:S(2)}) collective-permute-start(bf16[2,512,512]{2,1,0:T(8,128)(2,1)S(1)} %copy-done.8), channel_id=1, source_target_pairs={{0,2},{2,0},{1,3},{3,1},{4,6},{6,4},{5,7},{7,5},{8,10},{10,8},{9,1... | collective-permute-start | bytes 3145736 | tf_op jit(solution)/shard_map/ppermute | solution.py:14
  118.5 45.5 %collective-permute-start.4 = (bf16[2,512,512]{2,1,0:T(8,128)(2,1)S(1)}, bf16[2,512,512]{2,1,0:T(8,128)(2,1)S(1)}, u32[]{:S(2)}, u32[]{:S(2)}) collective-permute-start(bf16[2,512,512]{2,1,0:T(8,128)(2,1)S(1)} %copy-done.9), channel_id=1, source_target_pairs={{0,2},{2,0},{1,3},{3,1},{4,6},{6,4},{5,7},{7,5},{8,10},{10,8},{9,1... | collective-permute-start | bytes 3145736 | tf_op jit(solution)/shard_map/ppermute | solution.py:14
  166.2 7.2 %copy-start.5 = (bf16[2,1024,512]{2,1,0:T(8,128)(2,1)}, bf16[2,1024,512]{2,1,0:T(8,128)(2,1)S(1)}, u32[]{:S(2)}) copy-start(bf16[2,1024,512]{2,1,0:T(8,128)(2,1)S(1)} %get-tuple-element.22) | copy-start | bytes 6291460
  331.1 76.2 %copy-start = (f32[1024,512]{1,0:T(8,128)}, f32[1024,512]{1,0:T(8,128)S(1)}, u32[]{:S(2)}) copy-start(f32[1024,512]{1,0:T(8,128)S(1)} %fusion.17) | copy-start | bytes 6291460
  361.7 4.9 %copy-start.6 = (f32[512,512]{1,0:T(8,128)}, f32[512,512]{1,0:T(8,128)S(1)}, u32[]{:S(2)}) copy-start(f32[512,512]{1,0:T(8,128)S(1)} %fusion.48) | copy-start | bytes 3145732
  397.7 4.9 %copy-start.7 = (f32[512,512]{1,0:T(8,128)}, f32[512,512]{1,0:T(8,128)S(1)}, u32[]{:S(2)}) copy-start(f32[512,512]{1,0:T(8,128)S(1)} %fusion.41) | copy-start | bytes 3145732
  412.7 25.1 %collective-permute-start.5 = (f32[256,2,512]{2,0,1:T(8,128)S(1)}, f32[256,2,512]{2,0,1:T(8,128)}, u32[]{:S(2)}, u32[]{:S(2)}) collective-permute-start(f32[256,2,512]{2,0,1:T(8,128)S(1)} %fusion.32), channel_id=1, source_target_pairs={{0,2},{2,0},{1,3},{3,1},{4,6},{6,4},{5,7},{7,5},{8,10},{10,8},{9,1... | collective-permute-start | bytes 3145736 | tf_op jit(solution)/shard_map/ppermute | solution.py:14
  414.3 23.5 %copy-start.4 = (f32[512,1,512]{2,0,1:T(8,128)S(1)}, f32[512,1,512]{2,0,1:T(8,128)}, u32[]{:S(2)}) copy-start(f32[512,1,512]{2,0,1:T(8,128)} %fusion.26) | copy-start | bytes 3145732
  414.3 23.5 %copy-start.10 = (f32[2,256,512]{2,1,0:T(8,128)S(1)}, f32[2,256,512]{2,1,0:T(8,128)}, u32[]{:S(2)}) copy-start(f32[2,256,512]{2,1,0:T(8,128)} %param.19) | copy-start | bytes 3145732
Sparse Core Ops, SparseCore 0:
  115.1 213.3 all-reduce.1
Sparse Core Ops, SparseCore 1:
  117.1 179.1 all-gather.1

commit v2 on v1

--- a/solution.py
+++ b/solution.py
@@ -1,6 +1,10 @@
+import functools
+
 import jax
 import jax.numpy as jnp
 from jax import lax
+from jax.experimental import pallas as pl
+from jax.experimental.pallas import tpu as pltpu
 from jax.sharding import PartitionSpec as P
 
 BLK = 128
@@ -8,6 +12,7 @@
 CHILD = 2
 BF = jnp.bfloat16
 F32 = jnp.float32
+MESH = pl.DeviceIdType.MESH
 
 
 def swap(value, axis):
@@ -41,6 +46,320 @@
 
 def dot(a, b, dims):
     return lax.dot_general(a, b, (dims, ((), ())), preferred_element_type=F32)
+
+
+def exchange_kernel(
+    n,
+    sep,
+    panel,
+    side,
+    upper,
+    strip,
+    far,
+    summed,
+    side_full,
+    upper_full,
+    a_own,
+    a_peer,
+    p_send,
+    p_recv,
+    band,
+    far_low,
+    m_part,
+    m_recv,
+    total,
+    up_sem,
+    down_sem,
+    row_sem,
+    sub_send,
+    sub_recv,
+    x_send,
+    x_recv,
+    band_sem,
+    kid_send,
+    kid_recv,
+    m_send,
+    m_got,
+    g_send,
+    g_got,
+    local_sem,
+):
+    z = lax.axis_index("row")
+    c = lax.axis_index("col")
+    s = lax.axis_index("sub")
+    rows = sep.shape[0]
+    half = far.shape[1]
+    kid_rows = side.shape[1]
+    band_len = band.shape[0]
+    part = m_recv.shape[1]
+    sub_peer = {"sub": 1 - s}
+    col_peer = {"col": 1 - c}
+    root = z * 2 // n
+    base = pl.multiple_of((z - root * (n // 2)) * band_len, band_len)
+
+    barrier = pltpu.get_barrier_semaphore()
+    pl.semaphore_signal(barrier, inc=1, device_id=sub_peer, device_id_type=MESH)
+    pl.semaphore_signal(barrier, inc=1, device_id=col_peer, device_id_type=MESH)
+    for d in range(1, n):
+        pl.semaphore_signal(
+            barrier, inc=1, device_id={"row": lax.rem(z + d, n)}, device_id_type=MESH
+        )
+    pl.semaphore_wait(barrier, n + 1)
+
+    def piece(p, sub):
+        return strip.at[pl.ds(pl.multiple_of((p * 2 + sub) * rows, rows), rows), :]
+
+    def remote(src, dst, send, recv, to):
+        return pltpu.make_async_remote_copy(
+            src_ref=src, dst_ref=dst, send_sem=send, recv_sem=recv, device_id=to, device_id_type=MESH
+        )
+
+    def up(t, p, src):
+        return remote(src, piece(p, s), up_sem.at[t], row_sem.at[p], {"row": z + 1})
+
+    def down(t, p, src):
+        return remote(src, piece(p, s), down_sem.at[t], row_sem.at[p], {"row": z - 1})
+
+    def across(p, src):
+        return remote(src, piece(p, s), sub_send.at[p], sub_recv.at[p], sub_peer)
+
+    def from_peer(p):
+        return remote(piece(p, 1 - s), piece(p, 1 - s), sub_send.at[p], sub_recv.at[p], sub_peer)
+
+    def far_copy(j):
+        at = pl.ds(pl.multiple_of(j * rows, rows), rows)
+        return remote(p_send.at[at, :], p_recv.at[at, :], x_send.at[j], x_recv.at[j], col_peer)
+
+    def kid_copy(i):
+        src, dst = ((side, side_full), (upper, upper_full))[i]
+        place = dst.at[:, pl.ds(pl.multiple_of(c * kid_rows, kid_rows), kid_rows), :]
+        return remote(src, place, kid_send.at[i], kid_recv.at[i], col_peer)
+
+    def kid_own(i):
+        src, dst = ((side, side_full), (upper, upper_full))[i]
+        place = dst.at[:, pl.ds(pl.multiple_of(c * kid_rows, kid_rows), kid_rows), :]
+        return pltpu.make_async_copy(src, place, local_sem.at[4 + i])
+
+    def quarter(q):
+        return pl.ds(pl.multiple_of(q * part, part), part)
+
+    def m_copy(q):
+        return remote(
+            m_part.at[quarter(q), :], m_recv.at[z], m_send.at[q], m_got.at[z], {"row": q}
+        )
+
+    def m_from(p):
+        return remote(m_part.at[quarter(p), :], m_recv.at[p], m_send.at[p], m_got.at[p], {"row": p})
+
+    def g_copy(q):
+        return remote(total, summed.at[quarter(z), :], g_send.at[q], g_got.at[z], {"row": q})
+
+    def g_from(p):
+        return remote(total, summed.at[quarter(p), :], g_send.at[p], g_got.at[p], {"row": p})
+
+    load = pltpu.make_async_copy(sep, a_own, local_sem.at[0])
+    load.start()
+
+    @pl.when(z + 1 < n)
+    def _():
+        up(0, z, sep).start()
+
+    @pl.when(z >= 1)
+    def _():
+        down(0, z, sep).start()
+
+    across(z, sep).start()
+    own = pltpu.make_async_copy(sep, piece(z, s), local_sem.at[1])
+    own.start()
+    band_out = remote(
+        panel.at[pl.ds(base, band_len), :], band, band_sem.at[0], band_sem.at[1], col_peer
+    )
+    band_own = pltpu.make_async_copy(panel.at[pl.ds(base, band_len), :], band, local_sem.at[2])
+
+    @pl.when(c == root)
+    def _():
+        band_own.start()
+
+    tile = min(256, rows)
+    theirs = pl.ds(pl.multiple_of((1 - c) * half, half), half)
+    mine = pl.ds(pl.multiple_of(c * half, half), half)
+
+    def partial(src, dst, first, columns):
+        @pl.loop(0, rows // tile)
+        def _(i):
+            at = pl.ds(pl.multiple_of(i * tile, tile), tile)
+            to = pl.ds(pl.multiple_of(first * rows + i * tile, tile), tile)
+            dst[to, :] = jnp.dot(src[at, :], panel[:, columns], preferred_element_type=F32)
+
+    load.wait()
+    partial(a_own, p_send, s, theirs)
+    far_copy(s).start()
+
+    from_peer(z).wait_recv()
+    fetch = pltpu.make_async_copy(piece(z, 1 - s), a_peer, local_sem.at[3])
+    fetch.start()
+    fetch.wait()
+    partial(a_peer, p_send, 1 - s, theirs)
+    far_copy(1 - s).start()
+
+    @pl.when(c == root)
+    def _():
+        band_out.start()
+
+    for i in range(2):
+        kid_own(i).start()
+    partial(a_own, far, s, mine)
+    partial(a_peer, far, 1 - s, mine)
+
+    def arrive(t):
+        below, above = z - 1 - t, z + 1 + t
+
+        @pl.when(below >= 0)
+        def _():
+            up(t, below, piece(below, s)).wait_recv()
+            if t < n - 2:
+                @pl.when(z + 1 < n)
+                def _():
+                    up(t + 1, below, piece(below, s)).start()
+            across(below, piece(below, s)).start()
+
+        @pl.when(above < n)
+        def _():
+            down(t, above, piece(above, s)).wait_recv()
+            if t < n - 2:
+                @pl.when(z >= 1)
+                def _():
+                    down(t + 1, above, piece(above, s)).start()
+            across(above, piece(above, s)).start()
+
+    arrive(0)
+
+    for j in (s, 1 - s):
+        far_copy(j).wait_recv()
+
+        @pl.loop(0, rows // tile)
+        def _(i):
+            at = pl.ds(pl.multiple_of(j * rows + i * tile, tile), tile)
+            value = far[at, :] + p_recv[at, :]
+            far[at, :] = value
+            far_low[at, :] = value.astype(BF)
+
+    for i in range(2):
+        kid_copy(i).start()
+
+    @pl.when(c == root)
+    def _():
+        band_own.wait()
+        band_out.wait_send()
+
+    @pl.when(c != root)
+    def _():
+        band_out.wait_recv()
+
+    @pl.loop(0, n)
+    def _(q):
+        m_part[quarter(q), :] = lax.dot_general(
+            band[:, quarter(q)],
+            far_low[...],
+            (((0,), (0,)), ((), ())),
+            preferred_element_type=F32,
+        )
+
+    others = [lax.rem(z + d, n) for d in range(1, n)]
+    for q in others:
+        m_copy(q).start()
+    for t in range(1, n - 2):
+        arrive(t)
+    for p in others:
+        m_from(p).wait_recv()
+    value = m_part[quarter(z), :]
+    for p in others:
+        value = value + m_recv[p]
+    total[...] = value
+    for q in others:
+        g_copy(q).start()
+    keep = pltpu.make_async_copy(total, summed.at[quarter(z), :], local_sem.at[6])
+    keep.start()
+    arrive(n - 2)
+
+    own.wait()
+    keep.wait()
+    for i in range(2):
+        kid_own(i).wait()
+        kid_copy(i).wait_send()
+        kid_copy(i).wait_recv()
+    for j in (s, 1 - s):
+        far_copy(j).wait_send()
+    for p in others:
+        m_copy(p).wait_send()
+        g_copy(p).wait_send()
+        g_from(p).wait_recv()
+        from_peer(p).wait_recv()
+        across(p, piece(p, s)).wait_send()
+    across(z, sep).wait_send()
+    for t in range(n - 1):
+        @pl.when((z - t >= 0) & (z + 1 < n))
+        def _():
+            up(t, z - t, piece(z, s)).wait_send()
+
+        @pl.when((z + t < n) & (z >= 1))
+        def _():
+            down(t, z + t, piece(z, s)).wait_send()
+
+
+def exchange(sep, panel, side, upper):
+    n = lax.axis_size("row")
+    rows, strip_len = sep.shape
+    w1 = panel.shape[1]
+    half = w1 // 2
+    kids, kid_rows, w2 = side.shape
+    band_len = 2 * rows
+    part = w1 // n
+    any_spec = pl.BlockSpec(memory_space=pl.ANY)
+    vmem = pl.BlockSpec(memory_space=pltpu.VMEM)
+    dma = pltpu.SemaphoreType.DMA
+    full = jax.ShapeDtypeStruct((kids, 2 * kid_rows, w2), BF)
+    return pl.pallas_call(
+        functools.partial(exchange_kernel, n),
+        out_shape=(
+            jax.ShapeDtypeStruct((n * band_len, strip_len), BF),
+            jax.ShapeDtypeStruct((band_len, half), F32),
+            jax.ShapeDtypeStruct((w1, half), F32),
+            full,
+            full,
+        ),
+        in_specs=[any_spec, vmem, any_spec, any_spec],
+        out_specs=(any_spec, vmem, any_spec, any_spec, any_spec),
+        scratch_shapes=[
+            pltpu.VMEM((rows, strip_len), BF),
+            pltpu.VMEM((rows, strip_len), BF),
+            pltpu.VMEM((band_len, half), F32),
+            pltpu.VMEM((band_len, half), F32),
+            pltpu.VMEM((band_len, w1), BF),
+            pltpu.VMEM((band_len, half), BF),
+            pltpu.VMEM((w1, half), F32),
+            pltpu.VMEM((n, part, half), F32),
+            pltpu.VMEM((part, half), F32),
+            dma((n,)),
+            dma((n,)),
+            dma((n,)),
+            dma((n,)),
+            dma((n,)),
+            dma((2,)),
+            dma((2,)),
+            dma((2,)),
+            dma((2,)),
+            dma((2,)),
+            dma((n,)),
+            dma((n,)),
+            dma((n,)),
+            dma((n,)),
+            dma((8,)),
+        ],
+        compiler_params=pltpu.CompilerParams(
+            collective_id=0, has_side_effects=True, vmem_limit_bytes=48 * 2**20
+        ),
+    )(sep, panel, side, upper)
 
 
 def per_device(
@@ -70,9 +389,6 @@
     slice_two = w2 // cols_count
     zero = jnp.zeros((), BF)
 
-    whole_strip = lax.all_gather(sep_inverse, ("row", "sub"), axis=0, tiled=True)
-    own_rows = pair_gather(sep_inverse, "sub", 0)
-
     count_one = lax.dynamic_index_in_dim(parent_cols, sub_at, 0, keepdims=False)
     blocks_one = lax.dynamic_index_in_dim(parent_blocks, sub_at, 0, keepdims=False)
     live_rows = jnp.broadcast_to(blocks_one[:, None] > 0, (order // BLK, BLK)).reshape(order)
@@ -80,24 +396,29 @@
     live_one = jnp.arange(w1, dtype=jnp.int32) < count_one * BLK
     panel_one = jnp.where(strip_live[:, None] & live_one[None, :], parent_panel[0], zero)
 
-    root_col = row_at * cols_count // rows_count
-    offset = jnp.clip(row_at * band_len - root_col * strip_len, 0, strip_len - band_len)
-    sent_rows = lax.dynamic_slice_in_dim(panel_one, offset, band_len, 0)
-    if cols_count == 2:
-        mine_rows = jnp.where(col_at == root_col, sent_rows, swap(sent_rows, "col"))
+    if rows_count == 4 and cols_count == 2 and subs_count == 2:
+        whole_strip, far_rows, summed, side_rows, upper_rows = exchange(
+            sep_inverse, panel_one, child_separator, child_parent
+        )
+        far_block = far_rows.T
     else:
+        whole_strip = lax.all_gather(sep_inverse, ("row", "sub"), axis=0, tiled=True)
+        own_rows = pair_gather(sep_inverse, "sub", 0)
+        root_col = row_at * cols_count // rows_count
+        offset = jnp.clip(row_at * band_len - root_col * strip_len, 0, strip_len - band_len)
+        sent_rows = lax.dynamic_slice_in_dim(panel_one, offset, band_len, 0)
         mine_rows = spread_2(sent_rows, "col", root_col)
-    far_block = pair_scatter(dot(panel_one, own_rows, ((0,), (1,))), "col")
-    far_round = far_block.astype(BF)
-    partial_value = dot(mine_rows, far_round, ((0,), (1,)))
-    summed = lax.psum(partial_value, "row")
+        far_block = pair_scatter(dot(panel_one, own_rows, ((0,), (1,))), "col")
+        far_round = far_block.astype(BF)
+        partial_value = dot(mine_rows, far_round, ((0,), (1,)))
+        summed = lax.psum(partial_value, "row")
+        side_rows = pair_gather(child_separator, "col", 1)
+        upper_rows = pair_gather(child_parent, "col", 1)
     keep_cols = lax.dynamic_slice_in_dim(live_one, col_at * slice_one, slice_one, 0)
     pivot_one = jnp.where(live_one[:, None] & keep_cols[None, :], parent_pivot[0], F32(0.0))
     inverse_one = pivot_one + summed
     inverse_round = inverse_one.astype(BF)
 
-    side_rows = pair_gather(child_separator, "col", 1)
-    upper_rows = pair_gather(child_parent, "col", 1)
     first_kid = (row_at * subs_count + sub_at) * CHILD
     kid_cols = lax.dynamic_slice_in_dim(child_cols, first_kid, CHILD, 0)
     kid_blocks = lax.dynamic_slice_in_dim(child_blocks, first_kid, CHILD, 0)

time: 448 us -> 349 us (0.78)
  waiting for transfers between devices: 297 us -> 19 us
  Pallas kernels: 0 us -> 215 us
  between operations: 16.3 us -> 1.42 us
  matrix products: 54.7 us -> 41.5 us
  starting transfers between devices: 7.56 us -> 1.46 us
    pallas_call x0 -> x1, Pallas kernels: none -> 215 us  [exchange(): pl.pallas_call(functools.partial(exchange_kernel, n), out_shape=(jax.Shap...]
    psum x1 -> x0, waiting for transfers between devices: 154 us -> none  [per_device(): summed = lax.psum(partial_value, 'row')]
    ppermute x6 -> x1, waiting for transfers between devices: 143 us -> 19 us  [swap(): return lax.ppermute(value, axis, [(0, 1), (1, 0)])]
    dot_general x10 -> x8, matrix products: 52.9 us -> 38.1 us  [dot(): return lax.dot_general(a, b, (dims, ((), ())), preferred_element_type=F32)]
    ppermute x6 -> x1, starting transfers between devices: 7.3 us -> 1.46 us  [swap(): return lax.ppermute(value, axis, [(0, 1), (1, 0)])]
  transfers between devices with their start and end apart: 8 -> 1, of which waited for: 6 -> 1; matrix products, arithmetic and copies ran while one was open for 8% -> 1% of each run, Pallas kernels for 0% -> 0%
where the time goes in v2:
time: 349 us; the launch traced here: 348 us
  Pallas kernels  215 us (62%)
  local copies, waits for them, and re-layouts  50 us (14%)
  matrix products  41.5 us (12%)
  other arithmetic  19.3 us (6%)
  waiting for transfers between devices  19 us (5%)
    pallas_call x1, Pallas kernels, exchange(): pl.pallas_call(functools.partial(exchange_kernel, n), out_shape=(jax.Shap...  215 us
    dot_general x8, matrix products, dot(): return lax.dot_general(a, b, (dims, ((), ())), preferred_element_type=F32)  38.1 us
    gather x2, local copies, waits for them, and re-layouts, per_device(): chosen = jnp.take(whole_strip, picked_rows[k], axis=0)  33.5 us
    ppermute x1, waiting for transfers between devices, swap(): return lax.ppermute(value, axis, [(0, 1), (1, 0)])  19 us
  transfers between devices with their start and end apart: 1, of which 1 were waited for; matrix products, arithmetic and copies ran while one was open for 1% of the time, Pallas kernels for 0%

profile of v2, /device:TPU:0, one launch (start us, length us, event | category | flops | bytes accessed | tf_op | source)
XLA Modules:
  0.0 348.1 jit_solution(14013723916697906558)
XLA Ops:
  5.2 4.4 %and_select_fusion.1.panel = bf16[2048,1024]{1,0:T(8,128)(2,1)} fusion(bf16[1,2048,1024]{2,1,0:T(8,128)(2,1)} %param.13, pred[1024]{0:T(1024)(128)(4,1)S(1)} %iota_compare_fusion.1, pred[2048]{0:T(1024)(128)(4,1)S(1)} %dynamic_slice.42), kind=kLoop, calls=%fused_computation.3 | loop fusion | flops 4194304 | bytes 8391680 | tf_op jit(solution)/shard_map/jit(_where)/select_n | solution.py:397
  9.7 215.4 %shard_map.121 = (bf16[4096,2048]{1,0:T(8,128)(2,1)}, f32[1024,512]{1,0:T(8,128)S(1)}, f32[1024,512]{1,0:T(8,128)}, bf16[2,1024,512]{2,1,0:T(8,128)(2,1)}, bf16[2,1024,512]{2,1,0:T(8,128)(2,1)}) custom-call(bf16[512,2048]{1,0:T(8,128)(2,1)} %sep.1, bf16[2048,1024]{1,0:T(8,128)(2,1)} %and_select_fusion.1.panel, bf16[2,512,512]{2,1,0:T(8,128)(2,1)S(1)} %copy-done, ...), custom_call_target="tpu_custom_call" | custom-call | tf_op jit(solution)/shard_map/pallas_call | solution.py:322
  225.1 16.8 %gather_fusion.1 = bf16[1024,2048]{1,0:T(8,128)(2,1)} fusion(bf16[4096,2048]{1,0:T(8,128)(2,1)} %get-tuple-element.12, s32[1024]{0:T(1024)S(1)} %get-tuple-element.28), kind=kCustom, calls=%fused_computation.1.clone | custom fusion | bytes 8392704 | tf_op jit(solution)/shard_map/jit(_take)/gather | solution.py:448
  241.9 16.7 %gather_fusion = bf16[1024,2048]{1,0:T(8,128)(2,1)} fusion(bf16[4096,2048]{1,0:T(8,128)(2,1)} %get-tuple-element.12, s32[1024]{0:T(1024)S(1)} %get-tuple-element.29), kind=kCustom, calls=%fused_computation.clone | custom fusion | bytes 8392704 | tf_op jit(solution)/shard_map/jit(_take)/gather | solution.py:448
  258.6 2.5 broadcast_select_fusion
  261.1 1.4 fusion.75
  265.5 3.9 %fusion.10 = bf16[512,2048]{1,0:T(8,128)(2,1)} fusion(bf16[1024,2048]{1,0:T(8,128)(2,1)S(1)} %copy-done.5, pred[1024]{0:T(1024)(128)(4,1)S(1)} %get-tuple-element.26, bf16[2,1024,512]{2,1,0:T(8,128)(2,1)S(1)} %get-tuple-element.31), kind=kOutput, calls=%fused_computation.14 | convolution fusion | flops 2150629376 | bytes 7341056 | tf_op jit(solution)/shard_map/dot_general | solution.py:48
  269.4 7.7 %fusion.34 = f32[512,512]{1,0:T(8,128)} fusion(bf16[512,2048]{1,0:T(8,128)(2,1)} %fusion.10, bf16[1,2048,1024]{2,1,0:T(8,128)(2,1)} %param.13, pred[1024]{0:T(1024)(128)(4,1)S(1)} %iota_compare_fusion.1, pred[2048]{0:T(1024)(128)(4,1)S(1)} %dynamic_slice.42, bf16[2,1024,512]{2,1,0:T(8,128)(2,1)} %copy-done.4), kind=kOutput, calls=%fused_computation.47 | convolution fusion | flops 3226468352 | bytes 8391680 | tf_op jit(solution)/shard_map/dot_general | solution.py:48
  277.1 6.3 %fusion.7 = bf16[512,2048]{1,0:T(8,128)(2,1)} fusion(bf16[1024,2048]{1,0:T(8,128)(2,1)} %gather_fusion, pred[1024]{0:T(1024)(128)(4,1)S(1)} %get-tuple-element.27, bf16[2,1024,512]{2,1,0:T(8,128)(2,1)} %copy-done.3), kind=kOutput, calls=%fused_computation.13 | convolution fusion | flops 2150629376 | bytes 7341056 | tf_op jit(solution)/shard_map/dot_general | solution.py:48
  283.5 6.7 %fusion.41 = f32[512,512]{1,0:T(8,128)S(1)} fusion(bf16[512,2048]{1,0:T(8,128)(2,1)} %fusion.7, bf16[1,2048,1024]{2,1,0:T(8,128)(2,1)} %param.13, pred[1024]{0:T(1024)(128)(4,1)S(1)} %iota_compare_fusion.1, pred[2048]{0:T(1024)(128)(4,1)S(1)} %dynamic_slice.42, bf16[2,1024,512]{2,1,0:T(8,128)(2,1)} %copy-done.4), kind=kOutput, calls=%fused_computation.50 | convolution fusion | flops 3226468352 | bytes 8391680 | tf_op jit(solution)/shard_map/dot_general | solution.py:48
  290.2 1.3 copy.23
  291.5 2.6 copy.25
  294.1 3.4 convolution_convert_fusion.2
  299.6 2.3 fusion.77
  303.4 2.2 fusion.76
  305.7 3.9 %fusion.13 = f32[1024,512]{1,0:T(8,128)} fusion(f32[1024,512]{1,0:T(8,128)} %get-tuple-element.9, f32[1,1024,512]{2,1,0:T(8,128)} %param.14, pred[512]{0:T(512)(128)(4,1)S(1)} %dynamic_slice.40, pred[1024]{0:T(1024)(128)(4,1)S(1)} %iota_compare_fusion.1), kind=kLoop, calls=%fused_computation.21 | loop fusion | flops 1572864 | bytes 6292992 | tf_op jit(solution)/shard_map/add | solution.py:419
  309.5 4.0 %fusion.19 = f32[512,1,512]{2,0,1:T(8,128)S(1)} fusion(f32[512,512]{1,0:T(8,128)} %fusion.34, f32[512,512]{1,0:T(8,128)} %fusion.77, f32[512,512]{0,1:T(8,128)} %copy.25, bf16[1,1024,512]{2,1,0:T(8,128)(2,1)} %get-tuple-element.24, s32[]{:T(128)S(6)} %select_n.56, f32[1024,512]{1,0:T(8,128)} %fusion.13), kind=kOutput, calls=%fused_computation.31 | convolution fusion | flops 806879232 | bytes 7864324 | tf_op jit(solution)/shard_map/dot_general | solution.py:48
  313.5 4.9 %fusion.22 = f32[512,1,512]{2,0,1:T(8,128)} fusion(f32[512,512]{1,0:T(8,128)} %copy-done.6, f32[512,512]{1,0:T(8,128)} %fusion.76, f32[512,512]{0,1:T(8,128)} %copy.23, bf16[1,1024,512]{2,1,0:T(8,128)(2,1)} %get-tuple-element.25, s32[]{:T(128)S(6)} %select_n.56, f32[1024,512]{1,0:T(8,128)} %fusion.13), kind=kOutput, calls=%fused_computation.35 | convolution fusion | flops 806879232 | bytes 7864324 | tf_op jit(solution)/shard_map/dot_general | solution.py:48
  318.4 2.1 fusion.25
  320.5 1.5 collective-permute-start
  322.0 1.6 negate_bitcast_fusion
  323.6 3.0 copy.26
  326.6 19.0 %collective-permute-done = f32[256,2,512]{2,0,1:T(8,128)} collective-permute-done((f32[256,2,512]{2,0,1:T(8,128)}, f32[256,2,512]{2,0,1:T(8,128)}, u32[]{:S(2)}, u32[]{:S(2)}) %collective-permute-start) | collective-permute-done | bytes 1048608 | tf_op jit(solution)/shard_map/ppermute | solution.py:19
  345.7 2.4 fusion.29
  (39 shorter events, 10.5 us)
Async XLA Ops:
  5.2 4.5 %copy-start = (bf16[2,512,512]{2,1,0:T(8,128)(2,1)S(1)}, bf16[2,512,512]{2,1,0:T(8,128)(2,1)}, u32[]{:S(2)}) copy-start(bf16[2,512,512]{2,1,0:T(8,128)(2,1)} %side.1) | copy-start | bytes 3145732
  5.2 4.5 %copy-start.1 = (bf16[2,512,512]{2,1,0:T(8,128)(2,1)S(1)}, bf16[2,512,512]{2,1,0:T(8,128)(2,1)}, u32[]{:S(2)}) copy-start(bf16[2,512,512]{2,1,0:T(8,128)(2,1)} %upper.1) | copy-start | bytes 3145732
  261.1 2.1 copy-start.4
  261.1 3.1 copy-start.3
  261.1 4.4 %copy-start.5 = (bf16[1024,2048]{1,0:T(8,128)(2,1)S(1)}, bf16[1024,2048]{1,0:T(8,128)(2,1)}, u32[]{:S(2)}) copy-start(bf16[1024,2048]{1,0:T(8,128)(2,1)} %gather_fusion.1) | copy-start | bytes 12582916
  290.2 3.9 %copy-start.6 = (f32[512,512]{1,0:T(8,128)}, f32[512,512]{1,0:T(8,128)S(1)}, u32[]{:S(2)}) copy-start(f32[512,512]{1,0:T(8,128)S(1)} %fusion.41) | copy-start | bytes 3145732
  298.0 1.6 copy-start.9
  301.8 1.6 copy-start.8
  320.5 25.1 %collective-permute-start = (f32[256,2,512]{2,0,1:T(8,128)}, f32[256,2,512]{2,0,1:T(8,128)}, u32[]{:S(2)}, u32[]{:S(2)}) collective-permute-start(f32[256,2,512]{2,0,1:T(8,128)} %fusion.25), channel_id=1, source_target_pairs={{0,2},{2,0},{1,3},{3,1},{4,6},{6,4},{5,7},{7,5},{8,10},{10,8},{9,1... | collective-permute-start | bytes 3145736 | tf_op jit(solution)/shard_map/ppermute | solution.py:19
  323.6 22.1 %copy-start.2 = (f32[512,1,512]{2,0,1:T(8,128)S(1)}, f32[512,1,512]{2,0,1:T(8,128)}, u32[]{:S(2)}) copy-start(f32[512,1,512]{2,0,1:T(8,128)} %fusion.22) | copy-start | bytes 3145732
  323.6 22.1 %copy-start.7 = (f32[2,256,512]{2,1,0:T(8,128)S(1)}, f32[2,256,512]{2,1,0:T(8,128)}, u32[]{:S(2)}) copy-start(f32[2,256,512]{2,1,0:T(8,128)} %param.19) | copy-start | bytes 3145732

commit v3 on v2

--- a/solution.py
+++ b/solution.py
@@ -34,13 +34,13 @@
     )
 
 
-def pair_scatter(value, axis):
+def pair_scatter(value, axis, dim):
     if lax.axis_size(axis) != 2:
-        return lax.psum_scatter(value, axis, scatter_dimension=0, tiled=True)
-    half = value.shape[0] // 2
+        return lax.psum_scatter(value, axis, scatter_dimension=dim, tiled=True)
+    half = value.shape[dim] // 2
     at = lax.axis_index(axis)
-    sent = lax.dynamic_slice_in_dim(value, (1 - at) * half, half, 0)
-    kept = lax.dynamic_slice_in_dim(value, at * half, half, 0)
+    sent = lax.dynamic_slice_in_dim(value, (1 - at) * half, half, dim)
+    kept = lax.dynamic_slice_in_dim(value, at * half, half, dim)
     return kept + swap(sent, axis)
 
 
@@ -362,6 +362,74 @@
     )(sep, panel, side, upper)
 
 
+def child_kernel(blocks, *refs):
+    picked = refs[:P2A]
+    side, upper, near, panel, inverse, out, side_t, spread, weight, reach = refs[P2A:]
+    k = pl.program_id(0)
+    strip_blocks = spread.shape[0] // BLK
+    first = lax.axis_index("col") * strip_blocks
+    spread[...] = jnp.zeros_like(spread)
+    for j in range(P2A):
+        local = blocks[k, j] - first
+
+        @pl.when((local >= 0) & (local < strip_blocks))
+        def _():
+            at = pl.ds(pl.multiple_of(local * BLK, BLK), BLK)
+            spread[at, :] = side[0, j * BLK : (j + 1) * BLK, :]
+
+    side_t[...] = side[0].T
+    tile = 2 * BLK
+
+    @pl.loop(0, spread.shape[0] // tile)
+    def _(i):
+        at = pl.ds(pl.multiple_of(i * tile, tile), tile)
+        chosen = jnp.concatenate([ref[:, at] for ref in picked], axis=0)
+        weight[:, at] = jnp.dot(side_t[...], chosen, preferred_element_type=F32).astype(BF)
+        through = jnp.dot(panel[at, :], upper[0], preferred_element_type=F32)
+        reach[at, :] = (0.5 * spread[at, :].astype(F32) - through).astype(BF)
+
+    both = jnp.dot(weight[...], reach[...], preferred_element_type=F32)
+    left_par = jnp.dot(upper[0].T, inverse[...], preferred_element_type=F32).astype(BF)
+    par_term = jnp.dot(left_par, near[0], preferred_element_type=F32)
+    out[0] = both + both.T + par_term
+
+
+def child_terms(kid_blocks, strip, side, upper, panel, inverse):
+    kids, depth, w2 = side.shape
+    strip_len = strip.shape[1]
+    half = inverse.shape[1]
+    col_at = lax.axis_index("col")
+    near = lax.dynamic_slice_in_dim(upper, col_at * half, half, 1)
+
+    def picked_spec(j):
+        return pl.BlockSpec((BLK, strip_len), lambda k, blocks: (blocks[k, j], 0))
+
+    def kid_spec(rows):
+        return pl.BlockSpec((1, rows, w2), lambda k, blocks: (k, 0, 0))
+
+    def whole(a):
+        return pl.BlockSpec(a.shape, lambda k, blocks: (0, 0))
+
+    return pl.pallas_call(
+        child_kernel,
+        out_shape=jax.ShapeDtypeStruct((kids, w2, w2), F32),
+        grid_spec=pltpu.PrefetchScalarGridSpec(
+            num_scalar_prefetch=1,
+            grid=(kids,),
+            in_specs=[picked_spec(j) for j in range(P2A)]
+            + [kid_spec(depth), kid_spec(depth), kid_spec(half), whole(panel), whole(inverse)],
+            out_specs=kid_spec(w2),
+            scratch_shapes=[
+                pltpu.VMEM((w2, depth), BF),
+                pltpu.VMEM((strip_len, w2), BF),
+                pltpu.VMEM((w2, strip_len), BF),
+                pltpu.VMEM((strip_len, w2), BF),
+            ],
+        ),
+        compiler_params=pltpu.CompilerParams(vmem_limit_bytes=48 * 2**20),
+    )(kid_blocks, *([strip] * P2A), side, upper, near, panel, inverse)
+
+
 def per_device(
     sep_inverse,
     parent_panel,
@@ -408,7 +476,7 @@
         offset = jnp.clip(row_at * band_len - root_col * strip_len, 0, strip_len - band_len)
         sent_rows = lax.dynamic_slice_in_dim(panel_one, offset, band_len, 0)
         mine_rows = spread_2(sent_rows, "col", root_col)
-        far_block = pair_scatter(dot(panel_one, own_rows, ((0,), (1,))), "col")
+        far_block = pair_scatter(dot(panel_one, own_rows, ((0,), (1,))), "col", 0)
         far_round = far_block.astype(BF)
         partial_value = dot(mine_rows, far_round, ((0,), (1,)))
         summed = lax.psum(partial_value, "row")
@@ -423,38 +491,13 @@
     kid_cols = lax.dynamic_slice_in_dim(child_cols, first_kid, CHILD, 0)
     kid_blocks = lax.dynamic_slice_in_dim(child_blocks, first_kid, CHILD, 0)
     live_two = jnp.arange(w2, dtype=jnp.int32)[None, :] < kid_cols[:, None] * BLK
-    left_side = jnp.where(live_two[:, None, :], side_rows, zero)
-    right_side = jnp.where(live_two[:, None, :], upper_rows, zero)
-    strip_blocks = col_at * (strip_len // BLK) + jnp.arange(strip_len // BLK, dtype=jnp.int32)
-    block_hits = (kid_blocks[:, None, :] == strip_blocks[None, :, None]).astype(BF)
-    spread = jnp.einsum(
-        "kbp,kpiw->kbiw",
-        block_hits,
-        left_side.reshape(CHILD, P2A, BLK, w2),
-        preferred_element_type=F32,
+    terms = child_terms(
+        kid_blocks, whole_strip, side_rows, upper_rows, panel_one, inverse_round
     )
-    spread = spread.astype(BF).reshape(CHILD, strip_len, w2)
-
-    picked_rows = (
-        kid_blocks[:, :, None] * BLK + jnp.arange(BLK, dtype=jnp.int32)[None, None, :]
-    ).reshape(CHILD, P2A * BLK)
-
-    terms = []
-    for k in range(CHILD):
-        right_slice = lax.dynamic_slice_in_dim(right_side[k], col_at * slice_one, slice_one, 0)
-        left_par = dot(right_side[k], inverse_round, ((0,), (0,))).astype(BF)
-        par_term = dot(left_par, right_slice, ((1,), (0,)))
-        reach = dot(panel_one, right_side[k], ((1,), (0,))).astype(BF)
-        chosen = jnp.take(whole_strip, picked_rows[k], axis=0)
-        weight = dot(left_side[k], chosen, ((0,), (0,))).astype(BF)
-        sep_term = dot(weight, spread[k], ((1,), (0,)))
-        cross = dot(weight, reach, ((1,), (0,)))
-        terms.append(sep_term + par_term - cross - cross.T)
-    term_sum = jnp.stack(terms, axis=1)
-    summed_two = pair_scatter(term_sum, "col")
+    summed_two = pair_scatter(terms, "col", 1)
     keep_two = lax.dynamic_slice_in_dim(live_two, col_at * slice_two, slice_two, 1)
-    pivot_two = jnp.where(keep_two[:, :, None] & live_two[:, None, :], child_pivot, F32(0.0))
-    child_out = pivot_two + jnp.transpose(summed_two, (1, 0, 2))
+    keep_both = keep_two[:, :, None] & live_two[:, None, :]
+    child_out = jnp.where(keep_both, child_pivot + summed_two, F32(0.0))
     return (inverse_one[None], (-far_block)[None], child_out)
 
 

time: 349 us -> 282 us (0.81)
  matrix products: 41.5 us -> 0 us
  local copies, waits for them, and re-layouts: 50 us -> 8.81 us
  Pallas kernels: 215 us -> 238 us
  other arithmetic: 19.3 us -> 14.2 us
    dot_general x9 -> x0, matrix products: 41.5 us -> none  [the longest x8 38.1 us: dot(): return lax.dot_general(a, b, (dims, ((), ())), preferred_element_type=F32)]
    gather x2 -> x0, local copies, waits for them, and re-layouts: 33.5 us -> none  [per_device(): chosen = jnp.take(whole_strip, picked_rows[k], axis=0)]
    pallas_call x0 -> x1, Pallas kernels: none -> 22.7 us  [child_terms(): pl.pallas_call(child_kernel, out_shape=jax.ShapeDtypeStruct((kids, w2, w2...]
    add x4 -> x0, other arithmetic: 6.38 us -> none  [the longest x1 3.88 us: per_device(): inverse_one = pivot_one + summed]
    slice x4 -> x0, local copies, waits for them, and re-layouts: 4.19 us -> none  [the longest x3 2.78 us: per_device(): sep_term = dot(weight, spread[k], ((1,), (0,)))]
    dot_general x2 -> x0, local copies, waits for them, and re-layouts: 3.89 us -> none  [dot(): return lax.dot_general(a, b, (dims, ((), ())), preferred_element_type=F32)]
  transfers between devices with their start and end apart: 1 -> 1, of which waited for: 1 -> 1; matrix products, arithmetic and copies ran while one was open for 1% -> 2% of each run, Pallas kernels for 0% -> 0%
where the time goes in v3:
time: 282 us; the launch traced here: 281 us
  Pallas kernels  238 us (84%)
  waiting for transfers between devices  17.4 us (6%)
  other arithmetic  14.2 us (5%)
  local copies, waits for them, and re-layouts  8.81 us (3%)
    pallas_call x1, Pallas kernels, exchange(): pl.pallas_call(functools.partial(exchange_kernel, n), out_shape=(jax.Shap...  215 us
    pallas_call x1, Pallas kernels, child_terms(): pl.pallas_call(child_kernel, out_shape=jax.ShapeDtypeStruct((kids, w2, w2...  22.7 us
    ppermute x1, waiting for transfers between devices, swap(): return lax.ppermute(value, axis, [(0, 1), (1, 0)])  17.4 us
  transfers between devices with their start and end apart: 1, of which 1 were waited for; matrix products, arithmetic and copies ran while one was open for 2% of the time, Pallas kernels for 0%

profile of v3, /device:TPU:0, one launch (start us, length us, event | category | flops | bytes accessed | tf_op | source)
XLA Modules:
  0.0 281.4 jit_solution(11911311260083437091)
XLA Ops:
  0.6 0.0 copy-start
  0.7 1.2 dynamic_slice.32
  2.6 0.7 compare_bitcast_fusion
  3.3 0.1 broadcast_bitcast_fusion
  3.3 0.1 constant_dynamic-slice_fusion.2
  3.4 0.1 copy.15.blocks
  3.5 0.1 dynamic_slice.33
  3.6 4.4 %and_select_fusion.panel.refs_11_ = bf16[2048,1024]{1,0:T(8,128)(2,1)} fusion(bf16[1,2048,1024]{2,1,0:T(8,128)(2,1)} %param.11, pred[1024]{0:T(1024)(128)(4,1)S(1)} %iota_compare_fusion.1, pred[2048]{0:T(1024)(128)(4,1)S(1)} %dynamic_slice.35), kind=kLoop, calls=%fused_computation | loop fusion | flops 4194304 | bytes 8391680 | tf_op jit(solution)/shard_map/jit(_where)/select_n | solution.py:465
  8.0 0.0 copy-done.3
  8.0 215.4 %shard_map.121 = (bf16[4096,2048]{1,0:T(8,128)(2,1)}, f32[1024,512]{1,0:T(8,128)S(1)}, f32[1024,512]{1,0:T(8,128)}, bf16[2,1024,512]{2,1,0:T(8,128)(2,1)}, bf16[2,1024,512]{2,1,0:T(8,128)(2,1)}) custom-call(bf16[512,2048]{1,0:T(8,128)(2,1)} %sep.1, bf16[2048,1024]{1,0:T(8,128)(2,1)} %and_select_fusion.panel.refs_11_, bf16[2,512,512]{2,1,0:T(8,128)(2,1)S(1)} %copy-done.2, ...), custom_call_target="tpu_custom_call" | custom-call | tf_op jit(solution)/shard_map/pallas_call | solution.py:322
  223.4 0.0 copy-start.1
  223.4 1.3 copy-done.1
  224.7 1.4 constant_dynamic-slice_fusion.1.refs_10_
  226.2 0.5 copy-done.4
  226.6 3.3 %fusion.1 = (bf16[1024,512]{1,0:T(8,128)(2,1)S(1)}, f32[1,1024,512]{2,1,0:T(8,128)}) fusion(f32[1024,512]{1,0:T(8,128)} %get-tuple-element.8, f32[1,1024,512]{2,1,0:T(8,128)S(1)} %copy-done.4, pred[512]{0:T(512)(128)(4,1)S(1)} %dynamic_slice.33, pred[1024]{0:T(1024)(128)(4,1)S(1)} %iota_compare_fusion.1), kind=kLoop, calls=%fused_computation.5 | loop fusion | flops 2097152 | bytes 7341568 | tf_op jit(solution)/shard_map/convert_element_type | solution.py:488
  230.0 22.7 %shard_map.122 = f32[2,512,512]{2,1,0:T(8,128)S(1)} custom-call(s32[2,8]{1,0:T(2,128)S(1)} %copy.15.blocks, bf16[4096,2048]{1,0:T(8,128)(2,1)} %get-tuple-element.10.refs_0_.refs_1_.refs_2_.refs_3_.refs_4_.refs_5_.refs_6_.refs_7_, bf16[4096,2048]{1,0:T(8,128)(2,1)} %get-tuple-element.10.refs_0_.refs_1_.refs_2_.refs_3_.refs_4_.refs_5_.refs_6_.refs_7_, ...), custom_call_target="tpu_custom_call" | custom-call | tf_op jit(solution)/shard_map/pallas_call | solution.py:413
  252.7 1.0 constant_dynamic-slice_fusion
  253.8 1.4 collective-permute-start
  255.2 3.2 %negate_bitcast_fusion = f32[1,512,1024]{1,2,0:T(8,128)} fusion(f32[1024,512]{1,0:T(8,128)} %copy-done.1), kind=kLoop, calls=%fused_computation.3 | loop fusion | flops 524288 | bytes 4194304 | tf_op jit(solution)/shard_map/broadcast_in_dim | solution.py:501
  258.4 3.0 %copy.14 = f32[1,512,1024]{2,1,0:T(8,128)} copy(f32[1,512,1024]{1,2,0:T(8,128)} %negate_bitcast_fusion) | data formatting | bytes 4194304
  261.3 0.1 dynamic-slice_multiply_fusion
  261.4 0.1 iota_compare_fusion
  261.5 17.4 %collective-permute-done = f32[2,256,512]{2,1,0:T(8,128)} collective-permute-done((f32[2,256,512]{2,1,0:T(8,128)}, f32[2,256,512]{2,1,0:T(8,128)}, u32[]{:S(2)}, u32[]{:S(2)}) %collective-permute-start) | collective-permute-done | bytes 1048608 | tf_op jit(solution)/shard_map/ppermute | solution.py:19
  278.9 2.5 add_select_fusion
  (12 shorter events, 0.0 us)
Async XLA Ops:
  0.6 2.7 copy-start
  3.6 4.4 %copy-start.2 = (bf16[2,512,512]{2,1,0:T(8,128)(2,1)S(1)}, bf16[2,512,512]{2,1,0:T(8,128)(2,1)}, u32[]{:S(2)}) copy-start(bf16[2,512,512]{2,1,0:T(8,128)(2,1)} %side.1) | copy-start | bytes 3145732
  3.6 4.4 %copy-start.3 = (bf16[2,512,512]{2,1,0:T(8,128)(2,1)S(1)}, bf16[2,512,512]{2,1,0:T(8,128)(2,1)}, u32[]{:S(2)}) copy-start(bf16[2,512,512]{2,1,0:T(8,128)(2,1)} %upper.1) | copy-start | bytes 3145732
  223.4 1.3 copy-start.1
  224.7 1.9 copy-start.4
  253.8 25.2 %collective-permute-start = (f32[2,256,512]{2,1,0:T(8,128)}, f32[2,256,512]{2,1,0:T(8,128)}, u32[]{:S(2)}, u32[]{:S(2)}) collective-permute-start(f32[2,256,512]{2,1,0:T(8,128)} %constant_dynamic-slice_fusion), channel_id=1, source_target_pairs={{0,2},{2,0},{1,3},{3,1},{4,6},{6,4},{5,7},{7,5},{8,10},{10,8},{9,1... | collective-permute-start | bytes 3145736 | tf_op jit(solution)/shard_map/ppermute | solution.py:19
  258.4 3.0 %copy-start.6 = (s32[16]{0:T(128)S(1)}, s32[16]{0:T(128)}, u32[]{:S(2)}) copy-start(s32[16]{0:T(128)} %param.18) | copy-start | bytes 196
  258.4 20.6 %copy-start.5 = (f32[2,256,512]{2,1,0:T(8,128)S(1)}, f32[2,256,512]{2,1,0:T(8,128)}, u32[]{:S(2)}) copy-start(f32[2,256,512]{2,1,0:T(8,128)} %param.17) | copy-start | bytes 3145732

commit v4 on v3

--- a/solution.py
+++ b/solution.py
@@ -143,19 +143,24 @@
     def quarter(q):
         return pl.ds(pl.multiple_of(q * part, part), part)
 
-    def m_copy(q):
+    low = n // 2 - 1
+
+    def m_copy(o):
         return remote(
-            m_part.at[quarter(q), :], m_recv.at[z], m_send.at[q], m_got.at[z], {"row": q}
+            m_part.at[quarter(o), :], m_recv.at[z], m_send.at[o], m_got.at[z], {"row": o + low}
         )
 
     def m_from(p):
-        return remote(m_part.at[quarter(p), :], m_recv.at[p], m_send.at[p], m_got.at[p], {"row": p})
+        return remote(
+            m_part.at[quarter(0), :], m_recv.at[p], m_send.at[0], m_got.at[p], {"row": p}
+        )
 
     def g_copy(q):
-        return remote(total, summed.at[quarter(z), :], g_send.at[q], g_got.at[z], {"row": q})
-
-    def g_from(p):
-        return remote(total, summed.at[quarter(p), :], g_send.at[p], g_got.at[p], {"row": p})
+        return remote(total, summed.at[quarter(z - low), :], g_send.at[q], g_got.at[z], {"row": q})
+
+    def g_from(o):
+        p = o + low
+        return remote(total, summed.at[quarter(o), :], g_send.at[p], g_got.at[p], {"row": p})
 
     load = pltpu.make_async_copy(sep, a_own, local_sem.at[0])
     load.start()
@@ -256,34 +261,49 @@
     def _():
         band_out.wait_recv()
 
-    @pl.loop(0, n)
+    @pl.loop(0, band.shape[1] // tile)
     def _(q):
-        m_part[quarter(q), :] = lax.dot_general(
-            band[:, quarter(q)],
+        at = pl.ds(pl.multiple_of(q * tile, tile), tile)
+        m_part[at, :] = lax.dot_general(
+            band[:, at],
             far_low[...],
             (((0,), (0,)), ((), ())),
             preferred_element_type=F32,
         )
 
     others = [lax.rem(z + d, n) for d in range(1, n)]
-    for q in others:
-        m_copy(q).start()
+    for o in range(2):
+        @pl.when(z != o + low)
+        def _():
+            m_copy(o).start()
+
     for t in range(1, n - 2):
         arrive(t)
-    for p in others:
-        m_from(p).wait_recv()
-    value = m_part[quarter(z), :]
-    for p in others:
-        value = value + m_recv[p]
-    total[...] = value
-    for q in others:
-        g_copy(q).start()
-    keep = pltpu.make_async_copy(total, summed.at[quarter(z), :], local_sem.at[6])
-    keep.start()
+    owner = (z == low) | (z == low + 1)
+
+    @pl.when(owner)
+    def _():
+        for p in others:
+            m_from(p).wait_recv()
+
+        @pl.loop(0, part // tile)
+        def _(i):
+            at = pl.ds(pl.multiple_of(i * tile, tile), tile)
+            mine_at = pl.ds(pl.multiple_of((z - low) * part + i * tile, tile), tile)
+            value = m_part[mine_at, :]
+            for p in others:
+                value = value + m_recv[p, at, :]
+            total[at, :] = value
+
+        for q in others:
+            g_copy(q).start()
+        keep = pltpu.make_async_copy(total, summed.at[quarter(z - low), :], local_sem.at[6])
+        keep.start()
+        keep.wait()
+
     arrive(n - 2)
 
     own.wait()
-    keep.wait()
     for i in range(2):
         kid_own(i).wait()
         kid_copy(i).wait_send()
@@ -291,12 +311,20 @@
     for j in (s, 1 - s):
         far_copy(j).wait_send()
     for p in others:
-        m_copy(p).wait_send()
-        g_copy(p).wait_send()
-        g_from(p).wait_recv()
         from_peer(p).wait_recv()
         across(p, piece(p, s)).wait_send()
     across(z, sep).wait_send()
+    for o in range(2):
+        @pl.when(z != o + low)
+        def _():
+            m_copy(o).wait_send()
+            g_from(o).wait_recv()
+
+    @pl.when(owner)
+    def _():
+        for q in others:
+            g_copy(q).wait_send()
+
     for t in range(n - 1):
         @pl.when((z - t >= 0) & (z + 1 < n))
         def _():
@@ -314,7 +342,7 @@
     half = w1 // 2
     kids, kid_rows, w2 = side.shape
     band_len = 2 * rows
-    part = w1 // n
+    part = w1 // 2
     any_spec = pl.BlockSpec(memory_space=pl.ANY)
     vmem = pl.BlockSpec(memory_space=pltpu.VMEM)
     dma = pltpu.SemaphoreType.DMA

time: 282 us -> 262 us (0.929)
  Pallas kernels: 238 us -> 218 us
    pallas_call x1, Pallas kernels: 215 us -> 195 us  [exchange(): pl.pallas_call(functools.partial(exchange_kernel, n), out_shape=(jax.Shap...]
where the time goes in v4:
time: 262 us
  Pallas kernels  218 us (83%)
  waiting for transfers between devices  18.8 us (7%)
  other arithmetic  14.2 us (5%)
  local copies, waits for them, and re-layouts  8.81 us (3%)
    pallas_call x1, Pallas kernels, exchange(): pl.pallas_call(functools.partial(exchange_kernel, n), out_shape=(jax.Shap...  195 us
    pallas_call x1, Pallas kernels, child_terms(): pl.pallas_call(child_kernel, out_shape=jax.ShapeDtypeStruct((kids, w2, w2...  22.7 us
    ppermute x1, waiting for transfers between devices, swap(): return lax.ppermute(value, axis, [(0, 1), (1, 0)])  18.8 us
  transfers between devices with their start and end apart: 1, of which 1 were waited for; matrix products, arithmetic and copies ran while one was open for 2% of the time, Pallas kernels for 0%

profile of v4, /device:TPU:0, one launch (start us, length us, event | category | flops | bytes accessed | tf_op | source)
XLA Modules:
  0.0 261.6 jit_solution(2221814209248427530)
XLA Ops:
  0.6 0.0 copy-start
  0.7 1.2 dynamic_slice.32
  2.6 0.7 compare_bitcast_fusion
  3.3 0.1 broadcast_bitcast_fusion
  3.3 0.0 copy-done
  3.3 0.1 constant_dynamic-slice_fusion.2
  3.4 0.1 copy.15.blocks
  3.5 0.1 dynamic_slice.33
  3.6 4.4 %and_select_fusion.panel.refs_11_ = bf16[2048,1024]{1,0:T(8,128)(2,1)} fusion(bf16[1,2048,1024]{2,1,0:T(8,128)(2,1)} %param.11, pred[1024]{0:T(1024)(128)(4,1)S(1)} %iota_compare_fusion.1, pred[2048]{0:T(1024)(128)(4,1)S(1)} %dynamic_slice.35), kind=kLoop, calls=%fused_computation | loop fusion | flops 4194304 | bytes 8391680 | tf_op jit(solution)/shard_map/jit(_where)/select_n | solution.py:493
  8.0 195.5 %shard_map.121 = (bf16[4096,2048]{1,0:T(8,128)(2,1)}, f32[1024,512]{1,0:T(8,128)S(1)}, f32[1024,512]{1,0:T(8,128)}, bf16[2,1024,512]{2,1,0:T(8,128)(2,1)}, bf16[2,1024,512]{2,1,0:T(8,128)(2,1)}) custom-call(bf16[512,2048]{1,0:T(8,128)(2,1)} %sep.1, bf16[2048,1024]{1,0:T(8,128)(2,1)} %and_select_fusion.panel.refs_11_, bf16[2,512,512]{2,1,0:T(8,128)(2,1)S(1)} %copy-done.2, ...), custom_call_target="tpu_custom_call" | custom-call | tf_op jit(solution)/shard_map/pallas_call | solution.py:350
  203.5 0.0 copy-start.1
  203.5 1.3 copy-done.1
  204.8 1.4 constant_dynamic-slice_fusion.1.refs_10_
  206.3 0.5 copy-done.4
  206.7 3.3 %fusion.1 = (bf16[1024,512]{1,0:T(8,128)(2,1)S(1)}, f32[1,1024,512]{2,1,0:T(8,128)}) fusion(f32[1024,512]{1,0:T(8,128)} %get-tuple-element.8, f32[1,1024,512]{2,1,0:T(8,128)S(1)} %copy-done.4, pred[512]{0:T(512)(128)(4,1)S(1)} %dynamic_slice.33, pred[1024]{0:T(1024)(128)(4,1)S(1)} %iota_compare_fusion.1), kind=kLoop, calls=%fused_computation.5 | loop fusion | flops 2097152 | bytes 7341568 | tf_op jit(solution)/shard_map/convert_element_type | solution.py:516
  210.1 22.7 %shard_map.122 = f32[2,512,512]{2,1,0:T(8,128)S(1)} custom-call(s32[2,8]{1,0:T(2,128)S(1)} %copy.15.blocks, bf16[4096,2048]{1,0:T(8,128)(2,1)} %get-tuple-element.10.refs_0_.refs_1_.refs_2_.refs_3_.refs_4_.refs_5_.refs_6_.refs_7_, bf16[4096,2048]{1,0:T(8,128)(2,1)} %get-tuple-element.10.refs_0_.refs_1_.refs_2_.refs_3_.refs_4_.refs_5_.refs_6_.refs_7_, ...), custom_call_target="tpu_custom_call" | custom-call | tf_op jit(solution)/shard_map/pallas_call | solution.py:441
  232.8 1.0 constant_dynamic-slice_fusion
  233.9 0.2 collective-permute-start
  234.1 3.2 %negate_bitcast_fusion = f32[1,512,1024]{1,2,0:T(8,128)} fusion(f32[1024,512]{1,0:T(8,128)} %copy-done.1), kind=kLoop, calls=%fused_computation.3 | loop fusion | flops 524288 | bytes 4194304 | tf_op jit(solution)/shard_map/broadcast_in_dim | solution.py:529
  237.2 3.0 %copy.14 = f32[1,512,1024]{2,1,0:T(8,128)} copy(f32[1,512,1024]{1,2,0:T(8,128)} %negate_bitcast_fusion) | data formatting | bytes 4194304
  240.2 0.1 dynamic-slice_multiply_fusion
  240.3 0.1 iota_compare_fusion
  240.4 18.8 %collective-permute-done = f32[2,256,512]{2,1,0:T(8,128)} collective-permute-done((f32[2,256,512]{2,1,0:T(8,128)}, f32[2,256,512]{2,1,0:T(8,128)}, u32[]{:S(2)}, u32[]{:S(2)}) %collective-permute-start) | collective-permute-done | bytes 1048608 | tf_op jit(solution)/shard_map/ppermute | solution.py:19
  259.1 2.5 add_select_fusion
  (12 shorter events, 0.0 us)
Async XLA Ops:
  0.6 2.7 %copy-start = (s32[16,8]{0,1:T(8,128)S(1)}, s32[16,8]{0,1:T(8,128)}, u32[]{:S(2)}) copy-start(s32[16,8]{0,1:T(8,128)} %param.19) | copy-start | bytes 1540
  3.6 4.4 %copy-start.2 = (bf16[2,512,512]{2,1,0:T(8,128)(2,1)S(1)}, bf16[2,512,512]{2,1,0:T(8,128)(2,1)}, u32[]{:S(2)}) copy-start(bf16[2,512,512]{2,1,0:T(8,128)(2,1)} %side.1) | copy-start | bytes 3145732
  3.6 4.4 %copy-start.3 = (bf16[2,512,512]{2,1,0:T(8,128)(2,1)S(1)}, bf16[2,512,512]{2,1,0:T(8,128)(2,1)}, u32[]{:S(2)}) copy-start(bf16[2,512,512]{2,1,0:T(8,128)(2,1)} %upper.1) | copy-start | bytes 3145732
  203.5 1.3 copy-start.1
  204.8 1.9 copy-start.4
  233.9 25.2 %collective-permute-start = (f32[2,256,512]{2,1,0:T(8,128)}, f32[2,256,512]{2,1,0:T(8,128)}, u32[]{:S(2)}, u32[]{:S(2)}) collective-permute-start(f32[2,256,512]{2,1,0:T(8,128)} %constant_dynamic-slice_fusion), channel_id=1, source_target_pairs={{0,2},{2,0},{1,3},{3,1},{4,6},{6,4},{5,7},{7,5},{8,10},{10,8},{9,1... | collective-permute-start | bytes 3145736 | tf_op jit(solution)/shard_map/ppermute | solution.py:19
  237.2 3.0 %copy-start.6 = (s32[16]{0:T(128)S(1)}, s32[16]{0:T(128)}, u32[]{:S(2)}) copy-start(s32[16]{0:T(128)} %param.18) | copy-start | bytes 196
  237.2 21.9 %copy-start.5 = (f32[2,256,512]{2,1,0:T(8,128)S(1)}, f32[2,256,512]{2,1,0:T(8,128)}, u32[]{:S(2)}) copy-start(f32[2,256,512]{2,1,0:T(8,128)} %param.17) | copy-start | bytes 3145732
